TPU v7x, 256 devices: a whole 4x4x8 slice. The times are simulated.
256 devices in a mesh: tm: 64 (over x, y_hi, z), band: 4 (over y_lo, core).
Axes of the slice: x: 4, y: 4 (y_hi: 2, y_lo: 2; y = y_hi * 2 + y_lo), z: 8, core: 2. Of those that a mesh axis runs over, the one named last changes fastest.
Arguments:
- spectrum: bfloat16 [1024, 8192], P('tm', 'band'), may hold values from -60 to 60
- band_assign: int32 [2, 1024, 60], replicated, may hold values from 0 to 1, as said below
- split_weight: bfloat16 [1024, 2, 8, 384], P('band'), may hold values from -0.375 to 0.375
- qkv_weight: bfloat16 [384, 1536], replicated, may hold values from -8 to 8
- out_weight: bfloat16 [512, 384], replicated, may hold values from -0.25 to 0.25
- mask_weight: bfloat16 [1024, 2, 8, 384], P('band'), may hold values from -0.3125 to 0.3125
- mask_cotangent: bfloat16 [1024, 8192], P('tm', 'band'), may hold values from -6 to 6
Outputs:
- band_mask: float32 [1024, 8192], P('tm', 'band')
- qkv_grad: float32 [384, 1536], replicated
- out_grad: float32 [512, 384], replicated
Inputs may be any that keep to these rules, and one draw needn't show every extreme that they name: band_assign[0, f, b] = 1 where bin f lies on the rising side of band b and band_assign[1, f, b] = 1 where it lies on its falling side; each side is a run of consecutive bins, the falling side of band b is the rising side of band b + 1, and every bin lies on one or two sides.
All inputs are finite; a program needn't handle non-finite values.
Results may differ from a plain program's by a relative error of at most 0.02.
Values may be sent and summed in bfloat16 or wider, within the bound.
A program may use at most 128 MiB of HBM per device.

v0:
```python
import math

import jax
import jax.numpy as jnp
from jax import lax
from jax.sharding import PartitionSpec as P

HEADS = 8


EPSILON = 1e-05


def rms_scaled(hidden):
    values = hidden.astype(jnp.float32)
    return values * lax.rsqrt(jnp.mean(values * values, axis=-1, keepdims=True) + EPSILON)


def rms_back(hidden, upstream):
    values = hidden.astype(jnp.float32)
    inverse = lax.rsqrt(jnp.mean(values * values, axis=-1, keepdims=True) + EPSILON)
    inner = jnp.mean(upstream * values, axis=-1, keepdims=True)
    return inverse * upstream - values * (inverse * inverse * inverse) * inner


def rotary_tables(band_count, half_dim):
    position = jnp.arange(band_count).astype(jnp.float32)[:, None]
    frequency = jnp.exp(-math.log(10000.0) * jnp.arange(half_dim).astype(jnp.float32) / half_dim)[
        None, :
    ]
    angles = position * frequency
    return (jnp.cos(angles)[None, :, None, :], jnp.sin(angles)[None, :, None, :])


def rotate(vectors, rot_cos, rot_sin):
    half_dim = vectors.shape[-1] // 2
    front_half = vectors[..., :half_dim]
    back_half = vectors[..., half_dim:]
    return jnp.concatenate(
        [front_half * rot_cos - back_half * rot_sin, front_half * rot_sin + back_half * rot_cos],
        axis=-1,
    )


def unrotate(vectors, rot_cos, rot_sin):
    half_dim = vectors.shape[-1] // 2
    front_half = vectors[..., :half_dim]
    back_half = vectors[..., half_dim:]
    return jnp.concatenate(
        [front_half * rot_cos + back_half * rot_sin, back_half * rot_cos - front_half * rot_sin],
        axis=-1,
    )


def block_length():
    for candidate in (8, 4, 2, 1):
        return candidate
    return 1


def split_sums(spectrum_rows, split_part, onehot):
    row_count = spectrum_rows.shape[0]
    bin_count, bin_feats, model_width = (
        split_part.shape[0],
        split_part.shape[2],
        split_part.shape[3],
    )
    block_size = block_length()
    onehot_float = onehot.astype(jnp.float32)

    def one_block(block_rows):
        spec = block_rows.reshape(block_size, bin_count, bin_feats)
        contrib = jnp.einsum(
            "tfc,fscd->tfsd", spec, split_part, preferred_element_type=jnp.float32
        ).astype(jnp.bfloat16)
        summed = jnp.einsum("tfsd,sfb->tbd", contrib, onehot, preferred_element_type=jnp.float32)
        squares = jnp.sum(jnp.square(spec.astype(jnp.float32)), axis=2)
        energy = jnp.einsum("tf,sfb->tb", squares, onehot_float, precision=lax.Precision.HIGHEST)
        return (summed, energy)

    summed, energy = lax.map(
        one_block, spectrum_rows.reshape(row_count // block_size, block_size, -1)
    )
    return (
        summed.reshape(row_count, onehot.shape[2], model_width),
        energy.reshape(row_count, onehot.shape[2]),
    )


def mask_rows(normed_rows, mask_part, onehot, cover):
    row_count, band_count, model_width = normed_rows.shape
    bin_count, bin_feats = (mask_part.shape[0], mask_part.shape[2])
    block_size = block_length()

    def one_block(block_rows):
        picked = jnp.einsum(
            "tbd,sfb->tfsd", block_rows, onehot, preferred_element_type=jnp.float32
        ).astype(jnp.bfloat16)
        estimate = jnp.einsum(
            "tfsd,fscd->tfc", picked, mask_part, preferred_element_type=jnp.float32
        )
        return (estimate / cover[None, :, None]).reshape(block_size, bin_count * bin_feats)

    blocks = lax.map(
        one_block, normed_rows.reshape(row_count // block_size, block_size, band_count, model_width)
    )
    return blocks.reshape(row_count, bin_count * bin_feats)


def mask_grads(grad_rows, mask_part, onehot, cover):
    row_count = grad_rows.shape[0]
    bin_count, bin_feats, model_width = (mask_part.shape[0], mask_part.shape[2], mask_part.shape[3])
    block_size = block_length()

    def one_block(block_rows):
        scaled = (
            block_rows.reshape(block_size, bin_count, bin_feats).astype(jnp.float32)
            / cover[None, :, None]
        ).astype(jnp.bfloat16)
        picked = jnp.einsum(
            "tfc,fscd->tfsd", scaled, mask_part, preferred_element_type=jnp.float32
        ).astype(jnp.bfloat16)
        return jnp.einsum("tfsd,sfb->tbd", picked, onehot, preferred_element_type=jnp.float32)

    blocks = lax.map(one_block, grad_rows.reshape(row_count // block_size, block_size, -1))
    return blocks.reshape(row_count, onehot.shape[2], model_width)


def layer_forward(hidden_in, qkv_weight, out_weight, head_count):
    frame_count, band_count, model_width = hidden_in.shape
    inner_width = qkv_weight.shape[1] // 3
    head_dim = inner_width // head_count
    normed_in = rms_scaled(hidden_in).astype(jnp.bfloat16).reshape(-1, model_width)
    projected = jnp.dot(normed_in, qkv_weight, preferred_element_type=jnp.float32)
    projected = projected.reshape(frame_count, band_count, 3, head_count, head_dim)
    rot_cos, rot_sin = rotary_tables(band_count, head_dim // 2)
    queries = rotate(projected[:, :, 0], rot_cos, rot_sin).astype(jnp.bfloat16)
    key_vecs = rotate(projected[:, :, 1], rot_cos, rot_sin).astype(jnp.bfloat16)
    values = projected[:, :, 2].astype(jnp.bfloat16)
    scores = jnp.einsum(
        "tihe,tjhe->thij", queries, key_vecs, preferred_element_type=jnp.float32
    ) * head_dim ** (-0.5)
    attn_probs = jax.nn.softmax(scores, axis=-1)
    probs_bf = attn_probs.astype(jnp.bfloat16)
    attended = jnp.einsum("thij,tjhe->tihe", probs_bf, values, preferred_element_type=jnp.float32)
    attended = attended.astype(jnp.bfloat16).reshape(-1, inner_width)
    mixed = jnp.dot(attended, out_weight, preferred_element_type=jnp.float32)
    hidden_out = (hidden_in.astype(jnp.float32) + mixed.reshape(hidden_in.shape)).astype(
        jnp.bfloat16
    )
    return (hidden_out, (normed_in, queries, key_vecs, values, attn_probs, probs_bf, attended))


def attention_back(grad_flat, stored, out_weight):
    normed_in, queries, key_vecs, values, attn_probs, probs_bf, attended = stored
    band_count = queries.shape[1]
    head_dim = queries.shape[3]
    grad_attended = jnp.einsum(
        "ne,de->nd", grad_flat, out_weight, preferred_element_type=jnp.float32
    )
    grad_attended = grad_attended.astype(jnp.bfloat16).reshape(queries.shape)
    grad_probs = jnp.einsum(
        "tihe,tjhe->thij", grad_attended, values, preferred_element_type=jnp.float32
    )
    grad_values = jnp.einsum(
        "thij,tihe->tjhe", probs_bf, grad_attended, preferred_element_type=jnp.float32
    )
    grad_scores = (
        attn_probs
        * (grad_probs - jnp.sum(grad_probs * attn_probs, axis=-1, keepdims=True))
        * head_dim ** (-0.5)
    )
    grad_scores = grad_scores.astype(jnp.bfloat16)
    grad_queries = jnp.einsum(
        "thij,tjhe->tihe", grad_scores, key_vecs, preferred_element_type=jnp.float32
    )
    grad_keys = jnp.einsum(
        "thij,tihe->tjhe", grad_scores, queries, preferred_element_type=jnp.float32
    )
    rot_cos, rot_sin = rotary_tables(band_count, head_dim // 2)
    grad_projected = jnp.stack(
        [
            unrotate(grad_queries, rot_cos, rot_sin),
            unrotate(grad_keys, rot_cos, rot_sin),
            grad_values,
        ],
        axis=2,
    )
    grad_projected = grad_projected.astype(jnp.bfloat16).reshape(normed_in.shape[0], -1)
    return jnp.einsum("nd,ne->de", normed_in, grad_projected, preferred_element_type=jnp.float32)


def on_device(
    spectrum, band_assign, split_weight, qkv_weight, out_weight, mask_weight, mask_cotangent
):
    bin_count = split_weight.shape[0]
    bin_feats = split_weight.shape[2]
    model_width = split_weight.shape[3]
    onehot_all = band_assign.astype(jnp.bfloat16)
    band_sizes = bin_feats * jnp.sum(band_assign, axis=(0, 1)).astype(jnp.float32)
    onehot_own = lax.dynamic_slice_in_dim(
        onehot_all, lax.axis_index("band") * bin_count, bin_count, 1
    )
    cover_own = jnp.sum(onehot_own.astype(jnp.float32), axis=(0, 2))
    summed_part, energy_part = split_sums(spectrum, split_weight, onehot_own)
    summed, energy = (
        lax.psum_scatter(summed_part, "band", scatter_dimension=0, tiled=True),
        lax.psum_scatter(energy_part, "band", scatter_dimension=0, tiled=True),
    )
    hidden_in = (summed * lax.rsqrt(energy / band_sizes[None, :] + EPSILON)[:, :, None]).astype(
        jnp.bfloat16
    )
    hidden_out, stored = layer_forward(hidden_in, qkv_weight, out_weight, HEADS)
    normed_out = rms_scaled(hidden_out).astype(jnp.bfloat16)
    normed_all = lax.all_gather(normed_out, "band", axis=0, tiled=True)
    band_mask = mask_rows(normed_all, mask_weight, onehot_own, cover_own)
    grad_partial = mask_grads(mask_cotangent, mask_weight, onehot_own, cover_own)
    grad_normed = lax.psum_scatter(grad_partial, "band", scatter_dimension=0, tiled=True)
    grad_flat = rms_back(hidden_out, grad_normed).astype(jnp.bfloat16).reshape(-1, model_width)
    out_grad = jnp.einsum("nd,ne->de", stored[6], grad_flat, preferred_element_type=jnp.float32)
    qkv_grad = attention_back(grad_flat, stored, out_weight)
    qkv_grad, out_grad = lax.psum((qkv_grad, out_grad), ("tm", "band"))
    return (band_mask, qkv_grad, out_grad)


def solution(mesh):
    return jax.shard_map(
        on_device,
        mesh=mesh,
        in_specs=(
            P("tm", "band"),
            P(),
            P("band", None, None, None),
            P(),
            P(),
            P("band", None, None, None),
            P("tm", "band"),
        ),
        out_specs=(P("tm", "band"), P(), P()),
        check_vma=False,
    )
```

profile of v0, /device:TPU:1, one launch (start us, length us, event | category | flops | bytes accessed | tf_op | source)
XLA Modules:
  0.0 399.6 jit_solution(5693460215261702523)
XLA Ops:
  7.2 1.1 convert_reduce_fusion
  8.7 11.0 %while.34 = (s32[]{:T(128)}, f32[2,8,60,384]{3,2,1,0:T(8,128)S(1)}, f32[2,8,60]{2,1,0:T(8,128)S(1)}, bf16[2,8,2048]{2,1,0:T(8,128)(2,1)}, bf16[256,2,8,384]{3,2,...) while((s32[]{:T(128)}, f32[2,8,60,384]{3,2,1,0:T(8,128)S(1)}, ...), condition=%wide.region_3.0_spmd, body=%wide.region_1.3_spmd.sunk | while | flops 217004032 | bytes 10637417 | solution.py:81
  10.6 2.9 convert_bitcast_fusion.7
  16.1 2.9 convert_bitcast_fusion.7
  19.6 1.2 copy-done.2
  21.0 9.6 %while.36 = (s32[]{:T(128)}, f32[2,8,60,384]{3,2,1,0:T(8,128)S(1)}, bf16[2,8,2048]{2,1,0:T(8,128)(2,1)S(1)}, f32[256]{0:T(256)S(1)}, bf16[256,2,8,384]{3,2,1,0:T...) while((s32[]{:T(128)}, f32[2,8,60,384]{3,2,1,0:T(8,128)S(1)}, ...), condition=%wide.region_15.16_spmd, body=%wide.region_14.15_spmd.sunk | while | flops 215531520 | bytes 10847325 | solution.py:125
  22.3 2.8 convert_bitcast_fusion.9
  27.1 2.8 convert_bitcast_fusion.9
  30.7 1.1 copy-done.3
  31.9 2.2 reduce_sum.90
  34.2 2.4 copy.82
  36.6 8.8 %all-reduce = f32[16,60]{1,0:T(8,128)S(1)} all-reduce(f32[16,60]{1,0:T(8,128)S(1)} %bitcast.177), channel_id=3, replica_groups=mesh['tm'=64,'band'=4] {'band'}, use_global_device_ids=true, to_apply=%region_5.6.clone | all-reduce | flops 960 | bytes 7680
  47.5 4.3 %reduce-scatter.3.cloned.1.call-done = f32[4,60,384]{2,1,0:T(8,128)} async-done(((f32[16,60,384]{2,1,0:T(8,128)}), f32[4,60,384]{2,1,0:T(8,128)}) %reduce-scatter.3.cloned.1.call-update) | async-done | bytes 368656 | tf_op jit(solution)/shard_map/reduce_scatter | solution.py:207
  51.8 1.2 fusion.44
  53.9 2.4 fusion.53
  56.5 1.1 copy_bitcast_fusion
  57.7 1.6 subtract_convert_fusion.2
  60.4 2.2 copy.93
  62.6 2.3 pad_maximum_fusion.1
  64.8 2.1 copy.96
  67.0 3.4 fusion.62
  70.3 2.4 convolution_convert_fusion
  72.7 9.8 %reduce-scatter.5.cloned.1.call-done = f32[4,60,384]{2,1,0:T(8,128)} async-done(((f32[16,60,384]{2,1,0:T(8,128)}), f32[4,60,384]{2,1,0:T(8,128)}) %reduce-scatter.5.cloned.1.call-update) | async-done | bytes 368656 | tf_op jit(solution)/shard_map/reduce_scatter | solution.py:218
  82.5 1.6 multiply_reduce_fusion.2
  84.1 1.9 subtract_convert_fusion.4
  86.0 1.6 reshape.175
  87.7 1.9 convolution_convert_fusion.1
  89.6 2.0 reshape.176
  91.6 2.2 copy.99
  93.8 2.3 fusion.50
  96.1 1.8 fusion.47
  98.0 3.7 fusion.36
  101.7 3.7 fusion.35
  106.4 1.2 fusion.64
  107.7 1.7 copy.98
  109.3 1.7 copy.95
  112.9 1.1 convert_element_type.201
  114.1 9.2 %all_gather.3 = bf16[16,60,384]{2,1,0:T(8,128)(2,1)} all-gather(bf16[4,60,384]{2,1,0:T(8,128)(2,1)S(1)} %copy-done.13), channel_id=1, replica_groups=mesh['tm'=64,'band'=4] {'band'}, dimensions={0}, use_global_device_ids=true | all-gather | bytes 921600 | tf_op jit(solution)/shard_map/all_gather | solution.py:215
  123.2 1.9 fusion.63
  125.2 23.1 %while.35 = (s32[]{:T(128)}, f32[2,8,2048]{2,1,0:T(8,128)}, bf16[2,8,60,384]{3,2,1,0:T(8,128)(2,1)}, bf16[2,256,60]{1,2,0:T(8,128)(2,1)S(1)}, bf16[256,2,8,384]{...) while((s32[]{:T(128)}, f32[2,8,2048]{2,1,0:T(8,128)}, bf16[2,8,60,384]{3,2,1,0:T(8,128)(2,1)}, ...), condition=%wide.region_13.14_spmd, body=%wide.region_12.13_spmd.sunk | while | flops 215498752 | bytes 16643165 | solution.py:104
  125.2 2.0 convert_bitcast_fusion.8
  127.2 3.7 copy.149
  130.9 4.5 %divide_bitcast_fusion.2 = f32[8,256,8]{2,0,1:T(8,128)S(1)} fusion(bf16[8,256,2,384]{3,0,2,1:T(8,128)(2,1)} %copy.149, bf16[256,2,8,384]{3,2,1,0:T(8,128)(2,1)} %get-tuple-element.445, f32[256]{0:T(256)S(1)} %get-tuple-element.446), kind=kOutput, calls=%fused_computation.13.clone.1 | convolution fusion | flops 25182208 | bytes 6358016 | tf_op jit(solution)/shard_map/while/body/eval_jaxpr/tfsd,fscd->tfc/dot_general | solution.py:99
  136.7 2.0 convert_bitcast_fusion.8
  138.7 3.7 copy.149
  142.4 4.5 %divide_bitcast_fusion.2 = f32[8,256,8]{2,0,1:T(8,128)S(1)} fusion(bf16[8,256,2,384]{3,0,2,1:T(8,128)(2,1)} %copy.149, bf16[256,2,8,384]{3,2,1,0:T(8,128)(2,1)} %get-tuple-element.445, f32[256]{0:T(256)S(1)} %get-tuple-element.446), kind=kOutput, calls=%fused_computation.13.clone.1 | convolution fusion | flops 25182208 | bytes 6358016 | tf_op jit(solution)/shard_map/while/body/eval_jaxpr/tfsd,fscd->tfc/dot_general | solution.py:99
  148.3 240.6 %all-reduce.4.cloned.1.call-done = (f32[384,1536]{1,0:T(8,128)}, f32[512,384]{1,0:T(8,128)}) async-done(((f32[384,1536]{1,0:T(8,128)}, f32[512,384]{1,0:T(8,128)}), (f32[384,1536]{1,0:T(8,128)}, f32[512,384]{1,0:T(8,128)})) %all-reduce.4.cloned.1.call-update) | async-done | bytes 3145744 | tf_op jit(solution)/shard_map/psum | solution.py:222
  388.9 3.3 copy.183
  (104 shorter events, 19.8 us)
Async XLA Ops:
  7.2 75.3 %copy-start = (bf16[512,384]{1,0:T(8,128)(2,1)S(1)}, bf16[512,384]{1,0:T(8,128)(2,1)}, u32[]{:S(2)}) copy-start(bf16[512,384]{1,0:T(8,128)(2,1)} %param.17) | copy-start | bytes 1179652
  7.2 44.6 %reduce-scatter.3.cloned.1.call-start = ((), (), s32[]{:S(2)}) async-start(), calls=%async_computation.2 | async-start | bytes 1966080 | tf_op jit(solution)/shard_map/reduce_scatter | solution.py:207
  19.6 1.2 copy-start.2
  19.6 1.4 copy-start.15
  20.8 61.6 %reduce-scatter.5.cloned.1.call-start = ((), (), s32[]{:S(2)}) async-start(), calls=%async_computation.3 | async-start | bytes 1966080 | tf_op jit(solution)/shard_map/reduce_scatter | solution.py:218
  30.7 1.1 copy-start.3
  30.7 23.2 %copy-start.5 = (bf16[2,256,60]{1,2,0:T(8,128)(2,1)}, bf16[2,256,60]{1,2,0:T(8,128)(2,1)S(1)}, u32[]{:S(2)}) copy-start(bf16[2,256,60]{1,2,0:T(8,128)(2,1)S(1)} %get-tuple-element.466) | copy-start | bytes 184324
  30.7 14.7 %copy-start.21 = (u32[256]{0:T(256)S(1)}, u32[256]{0:T(256)}, u32[]{:S(2)}) copy-start(u32[256]{0:T(256)} %constant.78) | copy-start | bytes 3076
  31.8 357.0 %all-reduce.4.cloned.1.call-start = ((), (), s32[]{:S(2)}) async-start(), calls=%async_computation.4 | async-start | bytes 6291456 | tf_op jit(solution)/shard_map/psum | solution.py:222
  53.0 0.9 copy-start.10
  53.1 0.8 copy-start.4
  56.3 1.4 copy-start.16
  56.3 1.4 copy-start.18
  89.6 6.5 %copy-start.20 = (f32[4,8,60]{2,1,0:T(8,128)S(1)}, f32[4,8,60]{2,1,0:T(8,128)}, u32[]{:S(2)}) copy-start(f32[4,8,60]{2,1,0:T(8,128)} %get-tuple-element.260) | copy-start | bytes 23044
  96.1 1.9 copy-start.7
  98.0 3.7 copy-start.9
  101.7 4.1 %copy-start.8 = (bf16[4,8,64,60]{3,2,1,0:T(8,128)(2,1)S(1)}, bf16[4,8,64,60]{3,2,1,0:T(8,128)(2,1)}, u32[]{:S(2)}) copy-start(bf16[4,8,64,60]{3,2,1,0:T(8,128)(2,1)} %convolution_convert_fusion) | copy-start | bytes 737284
  101.7 4.8 %copy-start.11 = (bf16[240,384]{1,0:T(8,128)(2,1)S(1)}, bf16[240,384]{1,0:T(8,128)(2,1)}, u32[]{:S(2)}) copy-start(bf16[240,384]{1,0:T(8,128)(2,1)} %reshape.175) | copy-start | bytes 552964
  106.1 4.8 %copy-start.17 = (f32[60,32]{1,0:T(8,128)S(1)}, f32[60,32]{1,0:T(8,128)}, u32[]{:S(2)}) copy-start(f32[60,32]{1,0:T(8,128)} %get-tuple-element.258) | copy-start | bytes 23044
  106.1 4.8 %copy-start.19 = (f32[60,32]{1,0:T(8,128)S(1)}, f32[60,32]{1,0:T(8,128)}, u32[]{:S(2)}) copy-start(f32[60,32]{1,0:T(8,128)} %get-tuple-element.259) | copy-start | bytes 23044
  112.6 1.4 copy-start.13
  112.6 10.6 %copy-start.14 = (bf16[240,384]{1,0:T(8,128)(2,1)S(1)}, bf16[240,384]{1,0:T(8,128)(2,1)}, u32[]{:S(2)}) copy-start(bf16[240,384]{1,0:T(8,128)(2,1)} %reshape.172) | copy-start | bytes 552964
  123.2 1.9 copy-start.6
  388.9 3.3 copy-start.12
  388.9 4.2 %copy-start.1 = (bf16[512,384]{1,0:T(8,128)(2,1)S(1)}, bf16[512,384]{1,0:T(8,128)(2,1)}, u32[]{:S(2)}) copy-start(bf16[512,384]{1,0:T(8,128)(2,1)} %param.17) | copy-start | bytes 1179652
Sparse Core Ops, SparseCore 0:
  20.9 30.8 reduce-scatter.2
  54.9 27.4 reduce-scatter.4
  125.3 263.5 all-reduce.3
where the time goes:
time: 402 us; the launch traced here: 400 us
  waiting for transfers between devices  255 us (63%)
  matrix products  53.8 us (13%)
  local copies, waits for them, and re-layouts  43.1 us (11%)
  blocking collectives  18 us (4%)
  other arithmetic  14.8 us (4%)
  between operations  14.8 us (4%)
    psum x1, waiting for transfers between devices, on_device(): qkv_grad, out_grad = lax.psum((qkv_grad, out_grad), ('tm', 'band'))  241 us
    reduce_scatter x1, waiting for transfers between devices, on_device(): lax.psum_scatter(grad_partial, 'band', scatter_dimension=0, tiled=True)  9.77 us
    unnamed x48, local copies, waits for them, and re-layouts  9.53 us
    all_gather x1, blocking collectives, on_device(): normed_all = lax.all_gather(normed_out, 'band', axis=0, tiled=True)  9.17 us
    dot_general x2, matrix products, one_block(): jnp.einsum('tfsd,fscd->tfc', picked, mask_part, preferred_element_type=jn...  8.94 us
    unnamed x1, blocking collectives  8.82 us
  transfers between devices with their start and end apart: 3, of which 3 were waited for; matrix products, arithmetic and copies ran while one was open for 15% of the time, Pallas kernels for 0%

commit v1 on v0

v1 whole, which is shorter than its diff:
```python
import functools
import math

import jax
import jax.numpy as jnp
import numpy as np
from jax import lax
from jax.experimental import pallas as pl
from jax.experimental.pallas import tpu as pltpu
from jax.sharding import PartitionSpec as P

HEADS = 8
HEAD_DIM = 64
HALF = 32
D = 384
INNER = 512
BANDS = 60
PAD = 64
FEATS = 8
EPSILON = 1e-05
VMEM_BYTES = 50 * 1024 * 1024
BF16 = jnp.bfloat16
F32 = jnp.float32

NN = (((1,), (0,)), ((), ()))
NT = (((1,), (1,)), ((), ()))
TN = (((0,), (0,)), ((), ()))


def dot(left, right, dims=NN):
    return lax.dot_general(left, right, dims, preferred_element_type=F32)


def split_three(values):
    high = values.astype(BF16)
    rest = values - high.astype(F32)
    middle = rest.astype(BF16)
    low = (rest - middle.astype(F32)).astype(BF16)
    return high, middle, low


def iota(shape, dim):
    return lax.broadcasted_iota(jnp.int32, shape, dim)


def segment_masks(assign_ref, bin_count):
    first_bin = pl.multiple_of(lax.axis_index("band") * bin_count, bin_count)
    rising = assign_ref[0, pl.ds(first_bin, bin_count), :].astype(BF16)
    falling = assign_ref[1, pl.ds(first_bin, bin_count), :].astype(BF16)
    row, column = iota((PAD, BANDS), 0), iota((PAD, BANDS), 1)
    same = jnp.where(row == column, 1.0, 0.0).astype(BF16)
    last = jnp.where((row == BANDS) & (column == BANDS - 1), 1.0, 0.0).astype(BF16)
    segments = dot(same, rising, NT) + dot(last, falling, NT)
    bands = dot(same, rising, NT) + dot(same, falling, NT)
    width = bin_count * FEATS
    repeat = jnp.where(
        iota((bin_count, width), 1) // FEATS == iota((bin_count, width), 0), 1.0, 0.0
    ).astype(BF16)
    segment_mask = dot(segments.astype(BF16), repeat)
    band_mask = dot(bands.astype(BF16), repeat)
    cover = jnp.sum(band_mask, axis=0, keepdims=True)
    return segment_mask, band_mask, cover


def pack_weight(weight_ref, packed_ref):
    bin_count = weight_ref.shape[0]
    step = 32
    for first in range(0, bin_count, step):
        for side in range(2):
            block = weight_ref[first : first + step, side].astype(F32)
            packed_ref[first * FEATS : (first + step) * FEATS, side * D : (side + 1) * D] = (
                block.reshape(step * FEATS, D).astype(BF16)
            )


def masked_sums(rows_ref, mask, packed_ref, out_ref, masked_ref):
    quarter_rows = out_ref.shape[1]
    frames = quarter_rows // PAD
    in_band = iota((quarter_rows, 1), 0) % PAD < BANDS
    for quarter in range(out_ref.shape[0]):
        for frame in range(frames):
            row = rows_ref[quarter * frames + frame : quarter * frames + frame + 1, :]
            masked_ref[frame * PAD : (frame + 1) * PAD, :] = mask * row
        total = dot(masked_ref[...], packed_ref[...])
        shifted = pltpu.roll(total[:, D:], quarter_rows - 1, 0)
        out_ref[quarter] = jnp.where(in_band, total[:, :D] + shifted, 0.0).astype(BF16)


def split_kernel(
    spectrum_ref,
    cotangent_ref,
    assign_ref,
    split_ref,
    mask_ref,
    summed_ref,
    grad_ref,
    energy_ref,
    segment_ref,
    cover_ref,
    mask_packed_ref,
    split_packed_ref,
    masked_ref,
):
    bin_count = split_ref.shape[0]
    segment_mask, band_mask, cover = segment_masks(assign_ref, bin_count)
    segment_bf = segment_mask.astype(BF16)
    segment_ref[...] = segment_bf
    inverse = 1.0 / cover
    cover_ref[...] = inverse
    spectrum = spectrum_ref[...].astype(F32)
    band_bf = band_mask.astype(BF16)
    energy = jnp.zeros((spectrum.shape[0], PAD), F32)
    for term in split_three(spectrum * spectrum):
        energy += dot(term, band_bf, NT)
    energy_ref[...] = jnp.zeros_like(energy_ref)
    energy_ref[:, :PAD] = energy
    pack_weight(split_ref, split_packed_ref)
    masked_sums(spectrum_ref, segment_bf, split_packed_ref, summed_ref, masked_ref)
    pack_weight(mask_ref, mask_packed_ref)
    scaled = (segment_mask * inverse).astype(BF16)
    masked_sums(cotangent_ref, scaled, mask_packed_ref, grad_ref, masked_ref)


def remote(source, target, send, receive, index, device):
    return pltpu.make_async_remote_copy(
        src_ref=source,
        dst_ref=target,
        send_sem=send.at[index],
        recv_sem=receive.at[index],
        device_id=device,
        device_id_type=pl.DeviceIdType.MESH,
    )


def enter(devices):
    barrier = pltpu.get_barrier_semaphore()
    for device in devices:
        pl.semaphore_signal(
            barrier, inc=1, device_id=device, device_id_type=pl.DeviceIdType.MESH
        )
    pl.semaphore_wait(barrier, len(devices))


def reduce_kernel(
    summed_ref,
    grad_ref,
    energy_ref,
    summed_out,
    grad_out,
    energy_out,
    from_core,
    to_chip,
    from_chip,
    energies,
    send,
    receive,
):
    me_tm, me = lax.axis_index("tm"), lax.axis_index("band")
    chip, core = me // 2, me % 2
    other_core = (me_tm, chip * 2 + 1 - core)
    other_chip = (me_tm, (1 - chip) * 2 + core)
    peers = [(me_tm, lax.rem(me + step, 4)) for step in (1, 2, 3)]
    enter(peers)
    inputs, outputs = (summed_ref, grad_ref), (summed_out, grad_out)
    copies = []
    for slot, peer in enumerate(peers):
        copy = remote(energy_ref, energies.at[slot], send, receive, slot, peer)
        copy.start()
        copies.append(copy)
    first, second, across = [], [], []
    for item in range(2):
        copy = remote(
            inputs[item].at[(1 - chip) * 2 + 1 - core],
            from_core.at[item, 0],
            send,
            receive,
            3 + item,
            other_core,
        )
        copy.start()
        first.append(copy)
    for item in range(2):
        copy = remote(
            inputs[item].at[chip * 2 + 1 - core],
            from_core.at[item, 1],
            send,
            receive,
            5 + item,
            other_core,
        )
        copy.start()
        second.append(copy)
    for item in range(2):
        first[item].wait_recv()
        to_chip[item] = (
            inputs[item][(1 - chip) * 2 + core].astype(F32) + from_core[item, 0].astype(F32)
        ).astype(BF16)
        copy = remote(to_chip.at[item], from_chip.at[item], send, receive, 7 + item, other_chip)
        copy.start()
        across.append(copy)
    for copy in copies:
        copy.wait_recv()
    energy_out[...] = energy_ref[...] + energies[0] + energies[1] + energies[2]
    for item in range(2):
        second[item].wait_recv()
        across[item].wait_recv()
        outputs[item][...] = (
            inputs[item][chip * 2 + core].astype(F32) + from_core[item, 1].astype(F32)
        ) + from_chip[item].astype(F32)
    for copy in copies + first + second + across:
        copy.wait_send()


def layer_kernel(
    summed_ref,
    grad_ref,
    energy_ref,
    assign_ref,
    qkv_ref,
    out_weight_ref,
    table_ref,
    normed_ref,
    weight_grad_ref,
    probs_ref,
    heads_ref,
    attended_ref,
    grad_projected_ref,
):
    tokens = summed_ref.shape[0]
    frames = tokens // PAD
    me = lax.axis_index("band")
    sizes = FEATS * jnp.sum(
        (assign_ref[0] + assign_ref[1]).astype(F32), axis=0, keepdims=True
    )
    ratio = energy_ref[:, :BANDS] / jnp.maximum(sizes, 1.0)
    lane = iota((BANDS, tokens), 1)
    spread = jnp.where(lane % PAD == iota((BANDS, tokens), 0), 1.0, 0.0).astype(BF16)
    rows = energy_ref.shape[0]
    energy = jnp.zeros((rows, tokens), F32)
    for term in split_three(ratio):
        energy += dot(term, spread)
    mine = iota((rows, tokens), 0) == me * frames + iota((rows, tokens), 1) // PAD
    energy = jnp.sum(jnp.where(mine, energy, 0.0), axis=0, keepdims=True)
    in_band = iota((1, tokens), 1) % PAD < BANDS

    hidden_in = (jnp.transpose(summed_ref[...]) * lax.rsqrt(energy + EPSILON)).astype(BF16)
    hidden_in = hidden_in.astype(F32)
    normed_in = (
        hidden_in
        * lax.rsqrt(jnp.mean(hidden_in * hidden_in, axis=0, keepdims=True) + EPSILON)
    ).astype(BF16)
    projected = dot(qkv_ref[...], normed_in, TN)
    cos, sin = table_ref[:HALF, :], table_ref[HALF:, :]
    scale = HEAD_DIM**-0.5
    key_lane, query_lane = iota((tokens, tokens), 0), iota((tokens, tokens), 1)
    allowed = (key_lane // PAD == query_lane // PAD) & (key_lane % PAD < BANDS)
    bias = jnp.where(allowed, 0.0, -1e30)
    for head in range(HEADS):
        for part in range(2):
            base = part * INNER + head * HEAD_DIM
            front = projected[base : base + HALF]
            back = projected[base + HALF : base + HEAD_DIM]
            factor = scale if part == 0 else 1.0
            heads_ref[base : base + HALF, :] = ((front * cos - back * sin) * factor).astype(BF16)
            heads_ref[base + HALF : base + HEAD_DIM, :] = (
                (front * sin + back * cos) * factor
            ).astype(BF16)
    heads_ref[2 * INNER :, :] = projected[2 * INNER :].astype(BF16)

    def part_of(part, head):
        base = part * INNER + head * HEAD_DIM
        return heads_ref[base : base + HEAD_DIM, :]

    for head in range(HEADS):
        scores = dot(part_of(1, head), part_of(0, head), TN) + bias
        powers = jnp.exp(scores - jnp.max(scores, axis=0, keepdims=True))
        probs = powers / jnp.sum(powers, axis=0, keepdims=True)
        probs_ref[head] = probs
        attended_ref[head * HEAD_DIM : (head + 1) * HEAD_DIM, :] = dot(
            part_of(2, head), probs.astype(BF16)
        ).astype(BF16)
    mixed = dot(out_weight_ref[...], attended_ref[...], TN)
    hidden_out = (hidden_in + mixed).astype(BF16).astype(F32)
    inverse = lax.rsqrt(jnp.mean(hidden_out * hidden_out, axis=0, keepdims=True) + EPSILON)
    normed_out = jnp.where(in_band, hidden_out * inverse, 0.0)
    normed_ref[...] = jnp.transpose(normed_out).astype(BF16)

    upstream = jnp.transpose(grad_ref[...])
    inner = jnp.mean(upstream * hidden_out, axis=0, keepdims=True)
    grad_hidden = (
        inverse * upstream - hidden_out * (inverse * inverse * inverse) * inner
    ).astype(BF16)
    grad_attended = dot(out_weight_ref[...], grad_hidden).astype(BF16)
    out_grad = dot(attended_ref[...], grad_hidden, NT).astype(BF16)
    quarter = INNER // 4
    for block in range(4):
        weight_grad_ref[D:, block * D : (block + 1) * D] = out_grad[
            block * quarter : (block + 1) * quarter
        ]
    for head in range(HEADS):
        probs = probs_ref[head]
        grad_head = grad_attended[head * HEAD_DIM : (head + 1) * HEAD_DIM]
        grad_probs = dot(part_of(2, head), grad_head, TN)
        row_sum = jnp.sum(grad_probs * probs, axis=0, keepdims=True)
        grad_scores = (probs * (grad_probs - row_sum)).astype(BF16)
        grad_values = dot(grad_head, probs.astype(BF16), NT)
        grad_queries = dot(part_of(1, head), grad_scores) * scale
        grad_keys = dot(part_of(0, head), grad_scores, NT)
        for part, grad in ((0, grad_queries), (1, grad_keys)):
            base = part * INNER + head * HEAD_DIM
            front, back = grad[:HALF], grad[HALF:]
            grad_projected_ref[base : base + HALF, :] = (front * cos + back * sin).astype(BF16)
            grad_projected_ref[base + HALF : base + HEAD_DIM, :] = (
                back * cos - front * sin
            ).astype(BF16)
        base = 2 * INNER + head * HEAD_DIM
        grad_projected_ref[base : base + HEAD_DIM, :] = grad_values.astype(BF16)
    weight_grad_ref[:D, :] = dot(normed_in, grad_projected_ref[...], NT).astype(BF16)


def total_kernel(
    sizes,
    normed_ref,
    grad_ref,
    normed_out,
    grad_out,
    normed_all,
    gathered,
    core_in,
    pair_sum,
    first_in,
    first_sum,
    second_in,
    second_sum,
    depth_in,
    depth_all,
    second_all,
    send,
    receive,
):
    x_size, y_high, z_size = sizes
    y_size = y_high * 2
    me_tm, me = lax.axis_index("tm"), lax.axis_index("band")
    chip, core = me // 2, me % 2
    x = me_tm // (y_high * z_size)
    y = (me_tm // z_size) % y_high * 2 + chip
    z = me_tm % z_size

    def device(at_x, at_y, at_z, at_core):
        return ((at_x * y_high + at_y // 2) * z_size + at_z, (at_y % 2) * 2 + at_core)

    other_core = device(x, y, z, 1 - core)
    x_peers = [device(lax.rem(x + s, x_size), y, z, core) for s in range(1, x_size)]
    y_peers = [device(x, lax.rem(y + s, y_size), z, core) for s in range(1, y_size)]
    z_peers = [device(x, y, lax.rem(z + s, z_size), core) for s in range(1, z_size)]
    other_chip = (me_tm, (1 - chip) * 2 + core)
    enter([other_core] + x_peers + y_peers + z_peers)
    next_index = [0]
    started = []

    def begin(source, target, to):
        copy = remote(source, target, send, receive, next_index[0], to)
        next_index[0] += 1
        copy.start()
        started.append(copy)
        return copy

    half = grad_ref.shape[0] // 2
    columns = grad_ref.shape[1] // 2
    left, right = pl.ds(0, columns), pl.ds(columns, columns)

    normed_all[me] = normed_ref[...]
    pair_copy = begin(
        grad_ref.at[pl.ds(pl.multiple_of((1 - core) * half, half), half), :], core_in, other_core
    )
    to_chip = begin(normed_ref, normed_all.at[me], other_chip)
    to_core = begin(normed_ref, normed_all.at[me], other_core)

    pair_copy.wait_recv()
    own = pl.ds(pl.multiple_of(core * half, half), half)
    pair_sum[...] = (grad_ref[own, :].astype(F32) + core_in[...].astype(F32)).astype(BF16)

    axes = ((x, x_size, x_peers), (y, y_size, y_peers))
    rows = [half // x_size, half // y_size]
    firsts = ([], [])
    for step in range(max(x_size, y_size) - 1):
        for part in range(2):
            at, size, peers = axes[part]
            if step < size - 1:
                count = rows[part]
                there = pl.ds(pl.multiple_of(lax.rem(at + step + 1, size) * count, count), count)
                firsts[part].append(
                    begin(
                        pair_sum.at[there, (left, right)[part]],
                        first_in[part].at[step],
                        peers[step],
                    )
                )
    for part in range(2):
        at, size, peers = axes[part]
        count = rows[part]
        here = pl.ds(pl.multiple_of(at * count, count), count)
        total = pair_sum[here, (left, right)[part]].astype(F32)
        for step in range(size - 1):
            firsts[part][step].wait_recv()
            total += first_in[part][step].astype(F32)
        first_sum[part][...] = total.astype(BF16)

    last_rows = half // (x_size * y_size)
    seconds = ([], [])
    for part in range(2):
        at, size, peers = axes[1 - part]
        for step in range(size - 1):
            there = pl.ds(
                pl.multiple_of(lax.rem(at + step + 1, size) * last_rows, last_rows), last_rows
            )
            seconds[part].append(
                begin(first_sum[part].at[there, :], second_in[part].at[step], peers[step])
            )
    chunk_rows, chunk_columns = 8, columns // 2
    for part in range(2):
        at, size, peers = axes[1 - part]
        here = pl.ds(pl.multiple_of(at * last_rows, last_rows), last_rows)
        total = first_sum[part][here, :].astype(F32)
        for step in range(size - 1):
            seconds[part][step].wait_recv()
            total += second_in[part][step].astype(F32)
        if z_size == 1:
            second_all[part][here, :] = total.astype(BF16)
        else:
            for block in range(4):
                r, c = block // 2 * chunk_rows, block % 2 * chunk_columns
                second_sum[part * 4 + block] = total[r : r + chunk_rows, c : c + chunk_columns]

    if z_size > 1:
        depths = [
            begin(second_sum.at[lax.rem(z + s, z_size)], depth_in.at[s - 1], z_peers[s - 1])
            for s in range(1, z_size)
        ]
        total = second_sum[z]
        for step in range(z_size - 1):
            depths[step].wait_recv()
            total += depth_in[step]
        depth_all[z] = total
        backs = [begin(depth_all.at[z], depth_all.at[z], peer) for peer in z_peers]
        for copy in backs:
            copy.wait_recv()
        for part in range(2):
            at = axes[1 - part][0]
            here = pl.ds(pl.multiple_of(at * last_rows, last_rows), last_rows)
            rows_of = []
            for high in range(2):
                rows_of.append(
                    jnp.concatenate(
                        [depth_all[part * 4 + high * 2], depth_all[part * 4 + high * 2 + 1]], axis=1
                    )
                )
            second_all[part][here, :] = jnp.concatenate(rows_of, axis=0).astype(BF16)

    backs = ([], [])
    for part in range(2):
        at, size, peers = axes[1 - part]
        here = pl.ds(pl.multiple_of(at * last_rows, last_rows), last_rows)
        for peer in peers:
            backs[part].append(
                begin(second_all[part].at[here, :], second_all[part].at[here, :], peer)
            )
    to_chip.wait_recv()
    onward = begin(
        normed_all.at[(1 - chip) * 2 + core], normed_all.at[(1 - chip) * 2 + core], other_core
    )
    spread = ([], [])
    mirrored = []
    base = core * half
    for part in range(2):
        for copy in backs[part]:
            copy.wait_recv()
        at, size, peers = axes[part]
        count = rows[part]
        here = pl.ds(pl.multiple_of(base + at * count, count), count)
        target = gathered.at[here, (left, right)[part]]
        for peer in peers:
            spread[part].append(begin(second_all[part], target, peer))
        gathered[here, (left, right)[part]] = second_all[part][...]
        mirrored.append(begin(second_all[part], target, other_core))
    for step in range(max(x_size, y_size) - 1):
        for part in range(2):
            at, size, peers = axes[part]
            if step < size - 1:
                count = rows[part]
                spread[part][step].wait_recv()
                origin = lax.rem(at + size - step - 1, size)
                here = pl.ds(pl.multiple_of(base + origin * count, count), count)
                block = gathered.at[here, (left, right)[part]]
                mirrored.append(begin(block, block, other_core))
    to_core.wait_recv()
    onward.wait_recv()
    normed_out[...] = normed_all[...]
    for copy in mirrored:
        copy.wait_recv()
    grad_out[...] = gathered[...]
    for copy in started:
        copy.wait_send()


def mask_kernel(normed_ref, segment_ref, cover_ref, packed_ref, out_ref, pair_ref):
    quarter_rows = normed_ref.shape[1]
    frames = quarter_rows // PAD
    mask = segment_ref[...].astype(F32)
    inverse = cover_ref[...]
    for quarter in range(normed_ref.shape[0]):
        normed = normed_ref[quarter]
        pair_ref[:, :D] = normed
        pair_ref[:, D:] = pltpu.roll(normed.astype(F32), 1, 0).astype(BF16)
        estimate = dot(pair_ref[...], packed_ref[...], NT)
        for frame in range(frames):
            rows = estimate[frame * PAD : (frame + 1) * PAD]
            out_ref[quarter * frames + frame : quarter * frames + frame + 1, :] = (
                jnp.sum(rows * mask, axis=0, keepdims=True) * inverse
            )


VMEM = pl.BlockSpec(memory_space=pltpu.VMEM)


def call(kernel, outs, ins, scratch, **params):
    return pl.pallas_call(
        kernel,
        out_shape=outs,
        in_specs=[VMEM] * ins,
        out_specs=[VMEM] * len(outs),
        scratch_shapes=scratch,
        compiler_params=pltpu.CompilerParams(vmem_limit_bytes=VMEM_BYTES, **params),
    )


def rotary_table(tokens):
    position = (np.arange(tokens) % PAD).astype(np.float64)[None, :]
    frequency = np.exp(-math.log(10000.0) * np.arange(HALF) / HALF)[:, None]
    angles = position * frequency
    return np.concatenate([np.cos(angles), np.sin(angles)], axis=0).astype(np.float32)


def axis_sizes(tm_size):
    return {64: (4, 2, 8), 8: (4, 2, 1), 4: (4, 1, 1), 2: (2, 1, 1), 1: (1, 1, 1)}[tm_size]


def on_device(
    sizes, spectrum, band_assign, split_weight, qkv_weight, out_weight, mask_weight, mask_cotangent
):
    frames, width = spectrum.shape
    quarter = frames // 4 * PAD
    shape = jax.ShapeDtypeStruct
    summed, grad, energy, segment, cover, packed = call(
        split_kernel,
        [
            shape((4, quarter, D), BF16),
            shape((4, quarter, D), BF16),
            shape((frames, 128), F32),
            shape((PAD, width), BF16),
            shape((1, width), F32),
            shape((width, 2 * D), BF16),
        ],
        5,
        [pltpu.VMEM((width, 2 * D), BF16), pltpu.VMEM((quarter, width), BF16)],
    )(spectrum, mask_cotangent, band_assign, split_weight, mask_weight)
    summed, grad, energy = call(
        reduce_kernel,
        [shape((quarter, D), F32), shape((quarter, D), F32), shape((frames, 128), F32)],
        3,
        [
            pltpu.VMEM((2, 2, quarter, D), BF16),
            pltpu.VMEM((2, quarter, D), BF16),
            pltpu.VMEM((2, quarter, D), BF16),
            pltpu.VMEM((3, frames, 128), F32),
            pltpu.SemaphoreType.DMA((9,)),
            pltpu.SemaphoreType.DMA((9,)),
        ],
        collective_id=0,
        has_side_effects=True,
    )(summed, grad, energy)
    normed, weight_grad = call(
        layer_kernel,
        [shape((quarter, D), BF16), shape((INNER, 4 * D), BF16)],
        7,
        [
            pltpu.VMEM((HEADS, quarter, quarter), F32),
            pltpu.VMEM((3 * INNER, quarter), BF16),
            pltpu.VMEM((INNER, quarter), BF16),
            pltpu.VMEM((3 * INNER, quarter), BF16),
        ],
    )(
        summed,
        grad,
        energy,
        band_assign,
        qkv_weight,
        out_weight,
        jnp.asarray(rotary_table(quarter)),
    )
    x_size, y_high, z_size = sizes
    y_size = 2 * y_high
    half, columns = INNER // 2, 2 * D
    last = half // (x_size * y_size)
    copies = 64
    normed_all, weight_grad = call(
        functools.partial(total_kernel, sizes),
        [shape((4, quarter, D), BF16), shape((INNER, 4 * D), BF16)],
        2,
        [
            pltpu.VMEM((4, quarter, D), BF16),
            pltpu.VMEM((INNER, 4 * D), BF16),
            pltpu.VMEM((half, 4 * D), BF16),
            pltpu.VMEM((half, 4 * D), BF16),
            [
                pltpu.VMEM((max(x_size - 1, 1), half // x_size, columns), BF16),
                pltpu.VMEM((y_size - 1, half // y_size, columns), BF16),
            ],
            [
                pltpu.VMEM((half // x_size, columns), BF16),
                pltpu.VMEM((half // y_size, columns), BF16),
            ],
            [
                pltpu.VMEM((y_size - 1, last, columns), BF16),
                pltpu.VMEM((max(x_size - 1, 1), last, columns), BF16),
            ],
            pltpu.VMEM((8, 8, D), F32),
            pltpu.VMEM((7, 8, D), F32),
            pltpu.VMEM((8, 8, D), F32),
            [
                pltpu.VMEM((half // x_size, columns), BF16),
                pltpu.VMEM((half // y_size, columns), BF16),
            ],
            pltpu.SemaphoreType.DMA((copies,)),
            pltpu.SemaphoreType.DMA((copies,)),
        ],
        collective_id=1,
        has_side_effects=True,
    )(normed, weight_grad)
    band_mask = call(
        mask_kernel,
        [shape((frames, width), F32)],
        4,
        [pltpu.VMEM((quarter, 2 * D), BF16)],
    )(normed_all, segment, cover, packed)[0]
    qkv_grad = weight_grad[:D].astype(F32)
    out_grad = weight_grad[D:].reshape(INNER // 4, 4, D).transpose(1, 0, 2)
    return band_mask, qkv_grad, out_grad.reshape(INNER, D).astype(F32)


def solution(mesh):
    return jax.shard_map(
        functools.partial(on_device, axis_sizes(mesh.shape["tm"])),
        mesh=mesh,
        in_specs=(
            P("tm", "band"),
            P(),
            P("band", None, None, None),
            P(),
            P(),
            P("band", None, None, None),
            P("tm", "band"),
        ),
        out_specs=(P("tm", "band"), P(), P()),
        check_vma=False,
    )
```

time: 402 us -> 94.1 us (0.23)
  waiting for transfers between devices: 255 us -> 0 us
  Pallas kernels: 0 us -> 87.3 us
  matrix products: 53.8 us -> 0 us
  local copies, waits for them, and re-layouts: 43.1 us -> 4.06 us
  blocking collectives: 18 us -> 0 us
  between operations: 14.8 us -> 0.76 us
  other arithmetic: 14.8 us -> 1.76 us
    psum x1 -> x0, waiting for transfers between devices: 241 us -> none  [on_device(): qkv_grad, out_grad = lax.psum((qkv_grad, out_grad), ('tm', 'band'))]
    pallas_call x0 -> x5, Pallas kernels: none -> 87.3 us  [the longest x1 46.8 us: on_device(): call(functools.partial(total_kernel, sizes), [shape((4, quarter, D), BF16...]
    dot_general x24 -> x0, matrix products: 50.4 us -> none  [the longest x2 8.94 us: one_block(): jnp.einsum('tfsd,fscd->tfc', picked, mask_part, preferred_element_type=jn...]
    reduce_scatter x2 -> x0, waiting for transfers between devices: 14.1 us -> none  [the longest x1 9.77 us: on_device(): lax.psum_scatter(grad_partial, 'band', scatter_dimension=0, tiled=True)]
    convert_element_type x10 -> x2, local copies, waits for them, and re-layouts: 11.3 us -> 1.2 us  [on_device(): return (band_mask, qkv_grad, out_grad.reshape(INNER, D).astype(F32))]
    all_gather x1 -> x0, blocking collectives: 9.17 us -> none  [on_device(): normed_all = lax.all_gather(normed_out, 'band', axis=0, tiled=True)]
    unnamed x1 -> x0, blocking collectives: 8.82 us -> none
    reshape x7 -> x0, local copies, waits for them, and re-layouts: 8.08 us -> none  [the longest x2 4.18 us: attention_back(): grad_attended = grad_attended.astype(jnp.bfloat16).reshape(queries.shape)]
  transfers between devices with their start and end apart: 3 -> 0, of which waited for: 3 -> 0; matrix products, arithmetic and copies ran while one was open for 15% -> 0% of each run, Pallas kernels for 0% -> 0%
where the time goes in v1:
time: 94.1 us; the launch traced here: 93.9 us
  Pallas kernels  87.3 us (93%)
  local copies, waits for them, and re-layouts  4.06 us (4%)
  other arithmetic  1.76 us (2%)
    pallas_call x1, Pallas kernels, on_device(): call(functools.partial(total_kernel, sizes), [shape((4, quarter, D), BF16...  46.8 us
    pallas_call x1, Pallas kernels, on_device(): call(reduce_kernel, [shape((quarter, D), F32), shape((quarter, D), F32),...  15.7 us
    pallas_call x1, Pallas kernels, on_device(): call(split_kernel, [shape((4, quarter, D), BF16), shape((4, quarter, D),...  10.3 us
    pallas_call x1, Pallas kernels, on_device(): call(layer_kernel, [shape((quarter, D), BF16), shape((INNER, 4 * D), BF16...  8.4 us
    pallas_call x1, Pallas kernels, on_device(): call(mask_kernel, [shape((frames, width), F32)], 4, [pltpu.VMEM((quarter,...  6.13 us
    unnamed x13, local copies, waits for them, and re-layouts  2.85 us

profile of v1, /device:TPU:1, one launch (start us, length us, event | category | flops | bytes accessed | tf_op | source)
XLA Modules:
  0.0 93.9 jit_solution(1793693823107219517)
XLA Ops:
  0.6 0.0 copy-start.4
  0.6 0.0 copy-start.3
  0.7 1.4 %copy.11.assign_ref = s32[2,1024,60]{2,1,0:T(8,128)S(1)} copy(s32[2,1024,60]{1,0,2:T(2,128)} %param.9) | data formatting | bytes 983040 | tf_op args[1]
  2.1 0.0 copy-done.4
  2.1 0.0 copy-done.3
  2.1 0.0 copy-start.5
  2.1 10.3 %shard_map.103 = (bf16[4,256,384]{2,1,0:T(8,128)(2,1)S(1)}, bf16[4,256,384]{2,1,0:T(8,128)(2,1)S(1)}, f32[16,128]{1,0:T(8,128)S(1)}, bf16[64,2048]{1,0:T(8,128)(...) custom-call(bf16[16,2048]{1,0:T(8,128)(2,1)S(1)} %copy-done.3, bf16[16,2048]{1,0:T(8,128)(2,1)S(1)} %copy-done.4, ...), custom_call_target="tpu_custom_call" | custom-call | tf_op jit(solution)/shard_map/pallas_call | solution.py:554
  12.4 0.0 copy-start.1
  12.4 0.0 copy-start.2
  12.4 15.7 %shard_map.104 = (f32[256,384]{1,0:T(8,128)S(1)}, f32[256,384]{1,0:T(8,128)S(1)}, f32[16,128]{1,0:T(8,128)S(1)}) custom-call(bf16[4,256,384]{2,1,0:T(8,128)(2,1)S(1)} %get-tuple-element.16.summed_ref, bf16[4,256,384]{2,1,0:T(8,128)(2,1)S(1)} %get-tuple-element.17.grad_ref, f32[16,128]{1,0:T(8,128)S(1)} %get-tuple-element.18.energy_ref), custom_call_target="tpu_custom_call" | custom-call | tf_op jit(solution)/shard_map/pallas_call | solution.py:567
  28.1 0.0 copy-done.5
  28.1 0.0 copy-done.1
  28.2 0.0 copy-done.2
  28.2 8.4 %shard_map.105 = (bf16[256,384]{1,0:T(8,128)(2,1)S(1)}, bf16[512,1536]{1,0:T(8,128)(2,1)}) custom-call(f32[256,384]{1,0:T(8,128)S(1)} %get-tuple-element.19.summed_ref, f32[256,384]{1,0:T(8,128)S(1)} %get-tuple-element.20.grad_ref, f32[16,128]{1,0:T(8,128)S(1)} %get-tuple-element.21.energy_ref, s32[2,1024,60]{2,1,0:T(8,128)S(1)} %copy.11.assign_ref, ...), custom_call_target="tpu_custom_call" | custom-call | tf_op jit(solution)/shard_map/pallas_call | solution.py:582
  36.6 0.0 copy-start
  36.6 1.4 %copy-done = bf16[512,1536]{1,0:T(8,128)(2,1)S(1)} copy-done((bf16[512,1536]{1,0:T(8,128)(2,1)S(1)}, bf16[512,1536]{1,0:T(8,128)(2,1)}, u32[]{:S(2)}) %copy-start) | copy-done | bytes 1572888
  38.0 46.8 %shard_map.106 = (bf16[4,256,384]{2,1,0:T(8,128)(2,1)S(1)}, bf16[512,1536]{1,0:T(8,128)(2,1)S(1)}) custom-call(bf16[256,384]{1,0:T(8,128)(2,1)S(1)} %get-tuple-element.22.normed_ref, bf16[512,1536]{1,0:T(8,128)(2,1)S(1)} %copy-done), custom_call_target="tpu_custom_call" | custom-call | tf_op jit(solution)/shard_map/pallas_call | solution.py:606
  84.8 6.1 %shard_map.107 = f32[16,2048]{1,0:T(8,128)} custom-call(bf16[4,256,384]{2,1,0:T(8,128)(2,1)S(1)} %get-tuple-element.24.normed_ref, bf16[64,2048]{1,0:T(8,128)(2,1)S(1)} %get-tuple-element.25.segment_ref, f32[1,2048]{1,0:T(1,128)S(1)} %get-tuple-element.26.cover_ref, bf16[2048,768]{1,0:T(8,128)(2,1)} %get-tuple-element.27.packed_ref), custom_call_target="tpu_custom_call" | custom-call | tf_op jit(solution)/shard_map/pallas_call | solution.py:640
  90.9 0.1 slice_convert_fusion.1
  91.0 0.3 reshape.13
  91.3 0.9 copy.13
  92.2 1.7 %slice_convert_fusion = f32[384,1536]{1,0:T(8,128)} fusion(bf16[512,1536]{1,0:T(8,128)(2,1)S(1)} %get-tuple-element.28), kind=kLoop, calls=%fused_computation | loop fusion | flops 589824 | bytes 3538944 | tf_op jit(solution)/shard_map/convert_element_type | solution.py:646
Async XLA Ops:
  0.6 1.4 %copy-start.4 = (bf16[16,2048]{1,0:T(8,128)(2,1)S(1)}, bf16[16,2048]{1,0:T(8,128)(2,1)}, u32[]{:S(2)}) copy-start(bf16[16,2048]{1,0:T(8,128)(2,1)} %cotangent_ref.1) | copy-start | bytes 196612
  0.6 1.4 %copy-start.3 = (bf16[16,2048]{1,0:T(8,128)(2,1)S(1)}, bf16[16,2048]{1,0:T(8,128)(2,1)}, u32[]{:S(2)}) copy-start(bf16[16,2048]{1,0:T(8,128)(2,1)} %spectrum_ref.1) | copy-start | bytes 196612
  2.1 26.0 %copy-start.5 = (f32[64,256]{1,0:T(8,128)S(1)}, f32[64,256]{1,0:T(8,128)}, u32[]{:S(2)}) copy-start(f32[64,256]{1,0:T(8,128)} %constant.2.clone.table_ref) | copy-start | bytes 196612
  12.4 15.8 %copy-start.1 = (bf16[384,1536]{1,0:T(8,128)(2,1)S(1)}, bf16[384,1536]{1,0:T(8,128)(2,1)}, u32[]{:S(2)}) copy-start(bf16[384,1536]{1,0:T(8,128)(2,1)} %qkv_ref.1) | copy-start | bytes 3538948
  12.4 15.8 %copy-start.2 = (bf16[512,384]{1,0:T(8,128)(2,1)S(1)}, bf16[512,384]{1,0:T(8,128)(2,1)}, u32[]{:S(2)}) copy-start(bf16[512,384]{1,0:T(8,128)(2,1)} %out_weight_ref.1) | copy-start | bytes 1179652
  36.6 1.4 %copy-start = (bf16[512,1536]{1,0:T(8,128)(2,1)S(1)}, bf16[512,1536]{1,0:T(8,128)(2,1)}, u32[]{:S(2)}) copy-start(bf16[512,1536]{1,0:T(8,128)(2,1)} %get-tuple-element.23.grad_ref) | copy-start | bytes 4718596

commit v2 on v1

v2 whole, which is shorter than its diff:
```python
import functools
import math

import jax
import jax.numpy as jnp
import numpy as np
from jax import lax
from jax.experimental import pallas as pl
from jax.experimental.pallas import tpu as pltpu
from jax.sharding import PartitionSpec as P

HEADS = 8
HEAD_DIM = 64
HALF = 32
D = 384
INNER = 512
BANDS = 60
PAD = 64
FEATS = 8
EPSILON = 1e-05
VMEM_BYTES = 50 * 1024 * 1024
BF16 = jnp.bfloat16
F32 = jnp.float32

NN = (((1,), (0,)), ((), ()))
NT = (((1,), (1,)), ((), ()))
TN = (((0,), (0,)), ((), ()))


def dot(left, right, dims=NN):
    return lax.dot_general(left, right, dims, preferred_element_type=F32)


def split_three(values):
    high = values.astype(BF16)
    rest = values - high.astype(F32)
    middle = rest.astype(BF16)
    low = (rest - middle.astype(F32)).astype(BF16)
    return high, middle, low


def iota(shape, dim):
    return lax.broadcasted_iota(jnp.int32, shape, dim)


def segment_masks(assign_ref, first_bin, bin_count):
    rising = assign_ref[:, 0, pl.ds(first_bin, bin_count)].astype(F32).astype(BF16)
    falling = assign_ref[:, 1, pl.ds(first_bin, bin_count)].astype(F32).astype(BF16)
    row, column = iota((PAD, BANDS), 0), iota((PAD, BANDS), 1)
    same = jnp.where(row == column, 1.0, 0.0).astype(BF16)
    last = jnp.where((row == BANDS) & (column == BANDS - 1), 1.0, 0.0).astype(BF16)
    risen = dot(same, rising)
    segments = risen + dot(last, falling)
    bands = risen + dot(same, falling)
    width = bin_count * FEATS
    repeat = jnp.where(
        iota((bin_count, width), 1) // FEATS == iota((bin_count, width), 0), 1.0, 0.0
    ).astype(BF16)
    return dot(segments.astype(BF16), repeat), dot(bands.astype(BF16), repeat)


def pack_weight(weight_ref, packed_ref):
    bin_count = weight_ref.shape[0]
    step = 32
    for first in range(0, bin_count, step):
        for side in range(2):
            block = weight_ref[first : first + step, side].astype(F32)
            packed_ref[first * FEATS : (first + step) * FEATS, side * D : (side + 1) * D] = (
                block.reshape(step * FEATS, D).astype(BF16)
            )


def band_sums(rows_ref, first_row, mask_ref, packed_ref, masked_ref):
    tokens = masked_ref.shape[0]
    mask = mask_ref[...]
    for frame in range(tokens // PAD):
        row = rows_ref[pl.ds(first_row + frame, 1), :].astype(BF16)
        masked_ref[frame * PAD : (frame + 1) * PAD, :] = mask * row
    total = dot(masked_ref[...], packed_ref[...])
    shifted = pltpu.roll(total[:, D:], tokens - 1, 0)
    in_band = iota((tokens, 1), 0) % PAD < BANDS
    return jnp.where(in_band, total[:, :D] + shifted, 0.0).astype(BF16)


def whole_kernel(
    sizes,
    spectrum_ref,
    cotangent_ref,
    assign_ref,
    table_ref,
    split_hbm,
    mask_hbm,
    qkv_hbm,
    out_hbm,
    mask_out,
    qkv_out,
    out_out,
    split_raw,
    mask_raw,
    qkv_ref,
    out_weight_ref,
    split_packed,
    mask_packed,
    spectrum_rows,
    cotangent_rows,
    segment_ref,
    scaled_ref,
    inverse_ref,
    masked_ref,
    energy_ref,
    energies,
    parts,
    from_core,
    to_chip,
    from_chip,
    probs_ref,
    heads_ref,
    attended_ref,
    grad_projected_ref,
    grad_ref,
    normed_all,
    pair_ref,
    gathered,
    core_in,
    pair_sum,
    first_in,
    first_sum,
    second_in,
    second_sum,
    depth_in,
    depth_all,
    second_all,
    load,
    send,
    receive,
):
    x_size, y_high, z_size = sizes
    y_size = y_high * 2
    me_tm, me = lax.axis_index("tm"), lax.axis_index("band")
    chip, core = me // 2, me % 2
    x = me_tm // (y_high * z_size)
    y = (me_tm // z_size) % y_high * 2 + chip
    z = me_tm % z_size
    tokens = masked_ref.shape[0]
    frames = tokens // PAD

    def device(at_x, at_y, at_z, at_core):
        return ((at_x * y_high + at_y // 2) * z_size + at_z, (at_y % 2) * 2 + at_core)

    other_core = (me_tm, chip * 2 + 1 - core)
    other_chip = (me_tm, (1 - chip) * 2 + core)
    diagonal = (me_tm, (1 - chip) * 2 + 1 - core)
    x_peers = [device(lax.rem(x + s, x_size), y, z, core) for s in range(1, x_size)]
    y_peers = [device(x, lax.rem(y + s, y_size), z, core) for s in range(1, y_size)]
    z_peers = [device(x, y, lax.rem(z + s, z_size), core) for s in range(1, z_size)]
    everyone = [other_core, diagonal] + x_peers + y_peers + z_peers
    barrier = pltpu.get_barrier_semaphore()
    for peer in everyone:
        pl.semaphore_signal(barrier, inc=1, device_id=peer, device_id_type=pl.DeviceIdType.MESH)
    loads = []
    for index, (source, target) in enumerate(
        (
            (split_hbm, split_raw),
            (mask_hbm, mask_raw),
            (qkv_hbm, qkv_ref),
            (out_hbm, out_weight_ref),
        )
    ):
        copy = pltpu.make_async_copy(source, target, load.at[index])
        copy.start()
        loads.append(copy)
    next_index = [0]
    started = []

    def begin(source, target, to):
        index = next_index[0]
        next_index[0] += 1
        copy = pltpu.make_async_remote_copy(
            src_ref=source,
            dst_ref=target,
            send_sem=send.at[index],
            recv_sem=receive.at[index],
            device_id=to,
            device_id_type=pl.DeviceIdType.MESH,
        )
        copy.start()
        started.append(copy)
        return copy

    bin_count = split_raw.shape[0]
    first_bin = pl.multiple_of(me * bin_count, bin_count)
    segment_mask, band_mask = segment_masks(assign_ref, first_bin, bin_count)
    segment_ref[...] = segment_mask.astype(BF16)
    inverse = 1.0 / jnp.sum(band_mask, axis=0, keepdims=True)
    inverse_ref[...] = inverse
    scaled_ref[...] = (segment_mask * inverse).astype(BF16)
    spectrum = spectrum_ref[...].astype(F32)
    spectrum_rows[...] = spectrum
    cotangent_rows[...] = cotangent_ref[...].astype(F32)
    band_bf = band_mask.astype(BF16)
    energy = jnp.zeros((spectrum.shape[0], PAD), F32)
    for term in split_three(spectrum * spectrum):
        energy += dot(term, band_bf, NT)
    energy_ref[...] = jnp.zeros_like(energy_ref)
    energy_ref[:, :PAD] = energy

    quarters = [
        (1 - chip) * 2 + 1 - core,
        (1 - chip) * 2 + core,
        chip * 2 + 1 - core,
        me,
    ]
    energy_copies = []
    across = [None, None]
    seconds_in = [None, None]
    for item in range(2):
        loads[item].wait()
        raw, packed = ((split_raw, split_packed), (mask_raw, mask_packed))[item]
        rows_ref, mask_ref = ((spectrum_rows, segment_ref), (cotangent_rows, scaled_ref))[item]
        pack_weight(raw, packed)
        for slot in range(4):
            parts[item, slot] = band_sums(
                rows_ref, quarters[slot] * frames, mask_ref, packed, masked_ref
            )
            if item == 0 and slot == 0:
                pl.semaphore_wait(barrier, len(everyone))
                for index, peer in enumerate((other_core, other_chip, diagonal)):
                    energy_copies.append(begin(energy_ref, energies.at[index], peer))
            if slot == 0:
                first = begin(parts.at[item, 0], from_core.at[item, 0], other_core)
            if slot == 1:
                first.wait_recv()
                to_chip[item] = (
                    parts[item, 1].astype(F32) + from_core[item, 0].astype(F32)
                ).astype(BF16)
                across[item] = begin(to_chip.at[item], from_chip.at[item], other_chip)
            if slot == 2:
                seconds_in[item] = begin(parts.at[item, 2], from_core.at[item, 1], other_core)

    def reduced(item):
        seconds_in[item].wait_recv()
        across[item].wait_recv()
        own = parts[item, 3].astype(F32) + from_core[item, 1].astype(F32)
        return own + from_chip[item].astype(F32)

    for copy in energy_copies:
        copy.wait_recv()
    total_energy = energy_ref[...] + energies[0] + energies[1] + energies[2]
    both = (assign_ref[:, 0, :] + assign_ref[:, 1, :]).astype(F32).astype(BF16)
    bins = both.shape[1]
    band_sizes = FEATS * dot(jnp.ones((8, bins), BF16), both, NT)[:1]
    ratio = total_energy[:, :BANDS] / jnp.maximum(band_sizes, 1.0)
    lane = iota((BANDS, tokens), 1)
    spread = jnp.where(lane % PAD == iota((BANDS, tokens), 0), 1.0, 0.0).astype(BF16)
    rows = total_energy.shape[0]
    energy = jnp.zeros((rows, tokens), F32)
    for term in split_three(ratio):
        energy += dot(term, spread)
    mine = iota((rows, tokens), 0) == me * frames + iota((rows, tokens), 1) // PAD
    energy = jnp.sum(jnp.where(mine, energy, 0.0), axis=0, keepdims=True)
    in_band = iota((1, tokens), 1) % PAD < BANDS
    loads[2].wait()
    loads[3].wait()

    hidden_in = (jnp.transpose(reduced(0)) * lax.rsqrt(energy + EPSILON)).astype(BF16)
    hidden_in = hidden_in.astype(F32)
    normed_in = (
        hidden_in
        * lax.rsqrt(jnp.mean(hidden_in * hidden_in, axis=0, keepdims=True) + EPSILON)
    ).astype(BF16)
    projected = dot(qkv_ref[...], normed_in, TN)
    cos, sin = table_ref[:HALF, :], table_ref[HALF:, :]
    scale = HEAD_DIM**-0.5
    key_lane, query_lane = iota((tokens, tokens), 0), iota((tokens, tokens), 1)
    allowed = (key_lane // PAD == query_lane // PAD) & (key_lane % PAD < BANDS)
    bias = jnp.where(allowed, 0.0, -1e30)
    for head in range(HEADS):
        for part in range(2):
            base = part * INNER + head * HEAD_DIM
            front = projected[base : base + HALF]
            back = projected[base + HALF : base + HEAD_DIM]
            factor = scale if part == 0 else 1.0
            heads_ref[base : base + HALF, :] = ((front * cos - back * sin) * factor).astype(BF16)
            heads_ref[base + HALF : base + HEAD_DIM, :] = (
                (front * sin + back * cos) * factor
            ).astype(BF16)
    heads_ref[2 * INNER :, :] = projected[2 * INNER :].astype(BF16)

    def part_of(part, head):
        base = part * INNER + head * HEAD_DIM
        return heads_ref[base : base + HEAD_DIM, :]

    for head in range(HEADS):
        scores = dot(part_of(1, head), part_of(0, head), TN) + bias
        powers = jnp.exp(scores - jnp.max(scores, axis=0, keepdims=True))
        probs = powers / jnp.sum(powers, axis=0, keepdims=True)
        probs_ref[head] = probs
        attended_ref[head * HEAD_DIM : (head + 1) * HEAD_DIM, :] = dot(
            part_of(2, head), probs.astype(BF16)
        ).astype(BF16)
    mixed = dot(out_weight_ref[...], attended_ref[...], TN)
    hidden_out = (hidden_in + mixed).astype(BF16).astype(F32)
    inverse = lax.rsqrt(jnp.mean(hidden_out * hidden_out, axis=0, keepdims=True) + EPSILON)
    normed_out = jnp.where(in_band, hidden_out * inverse, 0.0)
    normed_all[me] = jnp.transpose(normed_out).astype(BF16)
    to_chip_rows = begin(normed_all.at[me], normed_all.at[me], other_chip)
    to_core_rows = begin(normed_all.at[me], normed_all.at[me], other_core)

    upstream = jnp.transpose(reduced(1))
    inner = jnp.mean(upstream * hidden_out, axis=0, keepdims=True)
    grad_hidden = (
        inverse * upstream - hidden_out * (inverse * inverse * inverse) * inner
    ).astype(BF16)
    grad_attended = dot(out_weight_ref[...], grad_hidden).astype(BF16)
    out_grad = dot(attended_ref[...], grad_hidden, NT).astype(BF16)
    quarter = INNER // 4
    for block in range(4):
        grad_ref[D:, block * D : (block + 1) * D] = out_grad[
            block * quarter : (block + 1) * quarter
        ]
    for head in range(HEADS):
        probs = probs_ref[head]
        grad_head = grad_attended[head * HEAD_DIM : (head + 1) * HEAD_DIM]
        grad_probs = dot(part_of(2, head), grad_head, TN)
        row_sum = jnp.sum(grad_probs * probs, axis=0, keepdims=True)
        grad_scores = (probs * (grad_probs - row_sum)).astype(BF16)
        grad_values = dot(grad_head, probs.astype(BF16), NT)
        grad_queries = dot(part_of(1, head), grad_scores) * scale
        grad_keys = dot(part_of(0, head), grad_scores, NT)
        for part, grad in ((0, grad_queries), (1, grad_keys)):
            base = part * INNER + head * HEAD_DIM
            front, back = grad[:HALF], grad[HALF:]
            grad_projected_ref[base : base + HALF, :] = (front * cos + back * sin).astype(BF16)
            grad_projected_ref[base + HALF : base + HEAD_DIM, :] = (
                back * cos - front * sin
            ).astype(BF16)
        base = 2 * INNER + head * HEAD_DIM
        grad_projected_ref[base : base + HEAD_DIM, :] = grad_values.astype(BF16)
    grad_ref[:D, :] = dot(normed_in, grad_projected_ref[...], NT).astype(BF16)

    def mask_rows(quarter):
        normed = normed_all[quarter]
        pair_ref[:, :D] = normed
        pair_ref[:, D:] = pltpu.roll(normed.astype(F32), 1, 0).astype(BF16)
        estimate = dot(pair_ref[...], mask_packed[...], NT)
        mask = segment_ref[...].astype(F32)
        for frame in range(frames):
            block = estimate[frame * PAD : (frame + 1) * PAD]
            mask_out[pl.ds(quarter * frames + frame, 1), :] = (
                jnp.sum(block * mask, axis=0, keepdims=True) * inverse_ref[...]
            )

    half = grad_ref.shape[0] // 2
    columns = grad_ref.shape[1] // 2
    left, right = pl.ds(0, columns), pl.ds(columns, columns)
    pair_copy = begin(
        grad_ref.at[pl.ds(pl.multiple_of((1 - core) * half, half), half), :], core_in, other_core
    )
    to_chip_rows.wait_recv()
    chip_rows = normed_all.at[(1 - chip) * 2 + core]
    onward = begin(chip_rows, chip_rows, other_core)
    mask_rows(me)
    pair_copy.wait_recv()
    own = pl.ds(pl.multiple_of(core * half, half), half)
    pair_sum[...] = (grad_ref[own, :].astype(F32) + core_in[...].astype(F32)).astype(BF16)

    axes = ((x, x_size, x_peers), (y, y_size, y_peers))
    counts = [half // x_size, half // y_size]
    firsts = ([], [])
    for step in range(max(x_size, y_size) - 1):
        for part in range(2):
            at, size, peers = axes[part]
            if step < size - 1:
                count = counts[part]
                there = pl.ds(pl.multiple_of(lax.rem(at + step + 1, size) * count, count), count)
                firsts[part].append(
                    begin(
                        pair_sum.at[there, (left, right)[part]],
                        first_in[part].at[step],
                        peers[step],
                    )
                )
    to_core_rows.wait_recv()
    mask_rows(chip * 2 + 1 - core)
    for part in range(2):
        at, size, peers = axes[part]
        count = counts[part]
        here = pl.ds(pl.multiple_of(at * count, count), count)
        total = pair_sum[here, (left, right)[part]].astype(F32)
        for step in range(size - 1):
            firsts[part][step].wait_recv()
            total += first_in[part][step].astype(F32)
        first_sum[part][...] = total.astype(BF16)

    last_rows = half // (x_size * y_size)
    seconds = ([], [])
    for part in range(2):
        at, size, peers = axes[1 - part]
        for step in range(size - 1):
            there = pl.ds(
                pl.multiple_of(lax.rem(at + step + 1, size) * last_rows, last_rows), last_rows
            )
            seconds[part].append(
                begin(first_sum[part].at[there, :], second_in[part].at[step], peers[step])
            )
    mask_rows((1 - chip) * 2 + core)
    chunk_rows, chunk_columns = 8, columns // 2
    for part in range(2):
        at, size, peers = axes[1 - part]
        here = pl.ds(pl.multiple_of(at * last_rows, last_rows), last_rows)
        total = first_sum[part][here, :].astype(F32)
        for step in range(size - 1):
            seconds[part][step].wait_recv()
            total += second_in[part][step].astype(F32)
        if z_size == 1:
            second_all[part][here, :] = total.astype(BF16)
        else:
            for block in range(4):
                r, c = block // 2 * chunk_rows, block % 2 * chunk_columns
                second_sum[part * 4 + block] = total[r : r + chunk_rows, c : c + chunk_columns]

    if z_size > 1:
        depths = [
            begin(second_sum.at[lax.rem(z + s, z_size)], depth_in.at[s - 1], z_peers[s - 1])
            for s in range(1, z_size)
        ]
    onward.wait_recv()
    mask_rows((1 - chip) * 2 + 1 - core)
    if z_size > 1:
        total = second_sum[z]
        for step in range(z_size - 1):
            depths[step].wait_recv()
            total += depth_in[step]
        depth_all[z] = total
        backs = [begin(depth_all.at[z], depth_all.at[z], peer) for peer in z_peers]
        for copy in backs:
            copy.wait_recv()
        for part in range(2):
            at = axes[1 - part][0]
            here = pl.ds(pl.multiple_of(at * last_rows, last_rows), last_rows)
            rows_of = []
            for high in range(2):
                rows_of.append(
                    jnp.concatenate(
                        [depth_all[part * 4 + high * 2], depth_all[part * 4 + high * 2 + 1]], axis=1
                    )
                )
            second_all[part][here, :] = jnp.concatenate(rows_of, axis=0).astype(BF16)

    backs = ([], [])
    for part in range(2):
        at, size, peers = axes[1 - part]
        here = pl.ds(pl.multiple_of(at * last_rows, last_rows), last_rows)
        for peer in peers:
            backs[part].append(
                begin(second_all[part].at[here, :], second_all[part].at[here, :], peer)
            )
    spread = ([], [])
    mirrored = []
    base = core * half
    for part in range(2):
        for copy in backs[part]:
            copy.wait_recv()
        at, size, peers = axes[part]
        count = counts[part]
        here = pl.ds(pl.multiple_of(base + at * count, count), count)
        target = gathered.at[here, (left, right)[part]]
        for peer in peers:
            spread[part].append(begin(second_all[part], target, peer))
        gathered[here, (left, right)[part]] = second_all[part][...]
        mirrored.append(begin(second_all[part], target, other_core))
    for step in range(max(x_size, y_size) - 1):
        for part in range(2):
            at, size, peers = axes[part]
            if step < size - 1:
                count = counts[part]
                spread[part][step].wait_recv()
                origin = lax.rem(at + size - step - 1, size)
                here = pl.ds(pl.multiple_of(base + origin * count, count), count)
                block = gathered.at[here, (left, right)[part]]
                mirrored.append(begin(block, block, other_core))
    for copy in mirrored:
        copy.wait_recv()
    qkv_out[...] = gathered[:D, :].astype(F32)
    for block in range(4):
        out_out[block * quarter : (block + 1) * quarter, :] = gathered[
            D:, block * D : (block + 1) * D
        ].astype(F32)
    for copy in started:
        copy.wait_send()


def rotary_table(tokens):
    position = (np.arange(tokens) % PAD).astype(np.float64)[None, :]
    frequency = np.exp(-math.log(10000.0) * np.arange(HALF) / HALF)[:, None]
    angles = position * frequency
    return np.concatenate([np.cos(angles), np.sin(angles)], axis=0).astype(np.float32)


def axis_sizes(tm_size):
    return {64: (4, 2, 8), 8: (4, 2, 1), 4: (4, 1, 1), 2: (2, 1, 1), 1: (1, 1, 1)}[tm_size]


def on_device(
    sizes, spectrum, band_assign, split_weight, qkv_weight, out_weight, mask_weight, mask_cotangent
):
    frames, width = spectrum.shape
    tokens = frames // 4 * PAD
    x_size, y_high, z_size = sizes
    y_size = 2 * y_high
    half, columns = INNER // 2, 2 * D
    last = half // (x_size * y_size)
    copies = 72

    def vmem(*shape, dtype=BF16):
        return pltpu.VMEM(shape, dtype)

    inside = pl.BlockSpec(memory_space=pltpu.VMEM)
    anywhere = pl.BlockSpec(memory_space=pl.ANY)
    assign = jnp.transpose(band_assign, (2, 0, 1))
    return pl.pallas_call(
        functools.partial(whole_kernel, sizes),
        out_shape=[
            jax.ShapeDtypeStruct((frames, width), F32),
            jax.ShapeDtypeStruct(qkv_weight.shape, F32),
            jax.ShapeDtypeStruct(out_weight.shape, F32),
        ],
        in_specs=[inside] * 4 + [anywhere] * 4,
        out_specs=[inside] * 3,
        scratch_shapes=[
            vmem(*split_weight.shape),
            vmem(*mask_weight.shape),
            vmem(*qkv_weight.shape),
            vmem(*out_weight.shape),
            vmem(width, 2 * D),
            vmem(width, 2 * D),
            vmem(frames, width, dtype=F32),
            vmem(frames, width, dtype=F32),
            vmem(PAD, width),
            vmem(PAD, width),
            vmem(1, width, dtype=F32),
            vmem(tokens, width),
            vmem(frames, 128, dtype=F32),
            vmem(3, frames, 128, dtype=F32),
            vmem(2, 4, tokens, D),
            vmem(2, 2, tokens, D),
            vmem(2, tokens, D),
            vmem(2, tokens, D),
            vmem(HEADS, tokens, tokens, dtype=F32),
            vmem(3 * INNER, tokens),
            vmem(INNER, tokens),
            vmem(3 * INNER, tokens),
            vmem(INNER, 4 * D),
            vmem(4, tokens, D),
            vmem(tokens, 2 * D),
            vmem(INNER, 4 * D),
            vmem(half, 4 * D),
            vmem(half, 4 * D),
            [
                vmem(max(x_size - 1, 1), half // x_size, columns),
                vmem(y_size - 1, half // y_size, columns),
            ],
            [vmem(half // x_size, columns), vmem(half // y_size, columns)],
            [vmem(y_size - 1, last, columns), vmem(max(x_size - 1, 1), last, columns)],
            vmem(8, 8, D, dtype=F32),
            vmem(7, 8, D, dtype=F32),
            vmem(8, 8, D, dtype=F32),
            [vmem(half // x_size, columns), vmem(half // y_size, columns)],
            pltpu.SemaphoreType.DMA((4,)),
            pltpu.SemaphoreType.DMA((copies,)),
            pltpu.SemaphoreType.DMA((copies,)),
        ],
        compiler_params=pltpu.CompilerParams(
            vmem_limit_bytes=VMEM_BYTES, collective_id=0, has_side_effects=True
        ),
    )(
        spectrum,
        mask_cotangent,
        assign,
        jnp.asarray(rotary_table(tokens)),
        split_weight,
        mask_weight,
        qkv_weight,
        out_weight,
    )


def solution(mesh):
    return jax.shard_map(
        functools.partial(on_device, axis_sizes(mesh.shape["tm"])),
        mesh=mesh,
        in_specs=(
            P("tm", "band"),
            P(),
            P("band", None, None, None),
            P(),
            P(),
            P("band", None, None, None),
            P("tm", "band"),
        ),
        out_specs=(P("tm", "band"), P(), P()),
        check_vma=False,
    )
```

time: 94.1 us -> 79.1 us (0.84)
  Pallas kernels: 87.3 us -> 67.5 us
  local copies, waits for them, and re-layouts: 4.06 us -> 10.6 us
  other arithmetic: 1.76 us -> 0 us
    pallas_call x5 -> x1, Pallas kernels: 87.3 us -> 67.5 us  [on_device(): pl.pallas_call(functools.partial(whole_kernel, sizes), out_shape=[jax.Sha...]
    unnamed x13 -> x15, local copies, waits for them, and re-layouts: 2.85 us -> 10.6 us
    convert_element_type x2 -> x0, other arithmetic: 1.76 us -> none  [the longest x1 1.69 us: on_device(): qkv_grad = weight_grad[:D].astype(F32)]
    convert_element_type x2 -> x0, local copies, waits for them, and re-layouts: 1.2 us -> none  [on_device(): return (band_mask, qkv_grad, out_grad.reshape(INNER, D).astype(F32))]
where the time goes in v2:
time: 79.1 us; the launch traced here: 78.7 us
  Pallas kernels  67.5 us (85%)
  local copies, waits for them, and re-layouts  10.6 us (13%)
    pallas_call x1, Pallas kernels, on_device(): pl.pallas_call(functools.partial(whole_kernel, sizes), out_shape=[jax.Sha...  67.5 us
    unnamed x15, local copies, waits for them, and re-layouts  10.6 us

profile of v2, /device:TPU:1, one launch (start us, length us, event | category | flops | bytes accessed | tf_op | source)
XLA Modules:
  0.0 78.7 jit_solution(10925201187462528729)
XLA Ops:
  0.6 0.0 copy-start
  0.6 1.3 %copy-done = bf16[384,1536]{1,0:T(8,128)(2,1)S(1)} copy-done((bf16[384,1536]{1,0:T(8,128)(2,1)S(1)}, bf16[384,1536]{1,0:T(8,128)(2,1)}, u32[]{:S(2)}) %copy-start) | copy-done | bytes 1179672
  1.9 0.0 copy-start.1
  1.9 1.0 %copy-done.1 = s32[2,1024,60]{1,0,2:T(2,128)S(1)} copy-done((s32[2,1024,60]{1,0,2:T(2,128)S(1)}, s32[2,1024,60]{1,0,2:T(2,128)}, u32[]{:S(2)}) %copy-start.1) | copy-done | bytes 491544
  2.9 0.0 copy-start.2
  2.9 1.0 %copy-done.2 = bf16[512,384]{1,0:T(8,128)(2,1)S(1)} copy-done((bf16[512,384]{1,0:T(8,128)(2,1)S(1)}, bf16[512,384]{1,0:T(8,128)(2,1)}, u32[]{:S(2)}) %copy-start.2) | copy-done | bytes 393240
  3.9 0.0 copy-start.3
  3.9 0.8 %copy-done.3 = bf16[16,2048]{1,0:T(8,128)(2,1)S(1)} copy-done((bf16[16,2048]{1,0:T(8,128)(2,1)S(1)}, bf16[16,2048]{1,0:T(8,128)(2,1)}, u32[]{:S(2)}) %copy-start.3) | copy-done | bytes 65560
  4.8 0.0 copy-start.4
  4.8 0.8 %copy-done.4 = bf16[16,2048]{1,0:T(8,128)(2,1)S(1)} copy-done((bf16[16,2048]{1,0:T(8,128)(2,1)S(1)}, bf16[16,2048]{1,0:T(8,128)(2,1)}, u32[]{:S(2)}) %copy-start.4) | copy-done | bytes 65560
  5.6 0.0 copy-start.5
  5.6 0.8 %copy-done.5 = f32[64,256]{1,0:T(8,128)S(1)} copy-done((f32[64,256]{1,0:T(8,128)S(1)}, f32[64,256]{1,0:T(8,128)}, u32[]{:S(2)}) %copy-start.5) | copy-done | bytes 65560
  6.5 67.5 %shard_map.103 = (f32[16,2048]{1,0:T(8,128)S(1)}, f32[384,1536]{1,0:T(8,128)}, f32[512,384]{1,0:T(8,128)S(1)}) custom-call(bf16[16,2048]{1,0:T(8,128)(2,1)S(1)} %copy-done.3, bf16[16,2048]{1,0:T(8,128)(2,1)S(1)} %copy-done.4, s32[60,2,1024]{2,1,0:T(2,128)S(1)} %bitcast.1, f32[64,256]{1,0:T(8,128)S(1)} %copy-done.5, bf16[256,2,8,384]{3,2,1,0:T(8,128)(2,1)} %split_hbm.1, ...), custom_call_target="tpu_custom_call" | custom-call | tf_op jit(solution)/shard_map/pallas_call | solution.py:521
  73.9 0.7 copy.14
  74.6 3.2 %copy.15 = f32[384,1536]{1,0:T(8,128)} copy(f32[384,1536]{1,0:T(8,128)} %get-tuple-element.7) | data formatting | bytes 4718592
  77.8 0.9 %copy.16 = f32[512,384]{1,0:T(8,128)} copy(f32[512,384]{1,0:T(8,128)S(1)} %get-tuple-element.8) | data formatting | bytes 1572864
Async XLA Ops:
  0.6 1.3 %copy-start = (bf16[384,1536]{1,0:T(8,128)(2,1)S(1)}, bf16[384,1536]{1,0:T(8,128)(2,1)}, u32[]{:S(2)}) copy-start(bf16[384,1536]{1,0:T(8,128)(2,1)} %qkv_hbm.1) | copy-start | bytes 3538948
  1.9 1.0 %copy-start.1 = (s32[2,1024,60]{1,0,2:T(2,128)S(1)}, s32[2,1024,60]{1,0,2:T(2,128)}, u32[]{:S(2)}) copy-start(s32[2,1024,60]{1,0,2:T(2,128)} %param.9) | copy-start | bytes 1474564
  2.9 1.0 %copy-start.2 = (bf16[512,384]{1,0:T(8,128)(2,1)S(1)}, bf16[512,384]{1,0:T(8,128)(2,1)}, u32[]{:S(2)}) copy-start(bf16[512,384]{1,0:T(8,128)(2,1)} %out_hbm.1) | copy-start | bytes 1179652
  3.9 0.8 %copy-start.3 = (bf16[16,2048]{1,0:T(8,128)(2,1)S(1)}, bf16[16,2048]{1,0:T(8,128)(2,1)}, u32[]{:S(2)}) copy-start(bf16[16,2048]{1,0:T(8,128)(2,1)} %spectrum_ref.1) | copy-start | bytes 196612
  4.8 0.8 %copy-start.4 = (bf16[16,2048]{1,0:T(8,128)(2,1)S(1)}, bf16[16,2048]{1,0:T(8,128)(2,1)}, u32[]{:S(2)}) copy-start(bf16[16,2048]{1,0:T(8,128)(2,1)} %cotangent_ref.1) | copy-start | bytes 196612
  5.6 0.8 %copy-start.5 = (f32[64,256]{1,0:T(8,128)S(1)}, f32[64,256]{1,0:T(8,128)}, u32[]{:S(2)}) copy-start(f32[64,256]{1,0:T(8,128)} %constant.2.clone.table_ref) | copy-start | bytes 196612

commit v3 on v2

--- a/solution.py
+++ b/solution.py
@@ -56,7 +56,7 @@
     repeat = jnp.where(
         iota((bin_count, width), 1) // FEATS == iota((bin_count, width), 0), 1.0, 0.0
     ).astype(BF16)
-    return dot(segments.astype(BF16), repeat), dot(bands.astype(BF16), repeat)
+    return dot(segments.astype(BF16), repeat), bands.astype(BF16), repeat
 
 
 def pack_weight(weight_ref, packed_ref):
@@ -84,17 +84,20 @@
 
 def whole_kernel(
     sizes,
-    spectrum_ref,
-    cotangent_ref,
-    assign_ref,
-    table_ref,
+    spectrum_hbm,
+    cotangent_hbm,
+    assign_hbm,
+    table_hbm,
     split_hbm,
     mask_hbm,
     qkv_hbm,
     out_hbm,
     mask_out,
-    qkv_out,
-    out_out,
+    gathered,
+    spectrum_ref,
+    cotangent_ref,
+    assign_ref,
+    table_ref,
     split_raw,
     mask_raw,
     qkv_ref,
@@ -120,7 +123,6 @@
     grad_ref,
     normed_all,
     pair_ref,
-    gathered,
     core_in,
     pair_sum,
     first_in,
@@ -160,10 +162,14 @@
     loads = []
     for index, (source, target) in enumerate(
         (
+            (assign_hbm, assign_ref),
+            (spectrum_hbm, spectrum_ref),
             (split_hbm, split_raw),
+            (cotangent_hbm, cotangent_ref),
             (mask_hbm, mask_raw),
             (qkv_hbm, qkv_ref),
             (out_hbm, out_weight_ref),
+            (table_hbm, table_ref),
         )
     ):
         copy = pltpu.make_async_copy(source, target, load.at[index])
@@ -187,22 +193,18 @@
         started.append(copy)
         return copy
 
+    def drain():
+        while started:
+            started.pop(0).wait_send()
+
     bin_count = split_raw.shape[0]
     first_bin = pl.multiple_of(me * bin_count, bin_count)
-    segment_mask, band_mask = segment_masks(assign_ref, first_bin, bin_count)
+    loads[0].wait()
+    segment_mask, bands, repeat = segment_masks(assign_ref, first_bin, bin_count)
     segment_ref[...] = segment_mask.astype(BF16)
-    inverse = 1.0 / jnp.sum(band_mask, axis=0, keepdims=True)
-    inverse_ref[...] = inverse
-    scaled_ref[...] = (segment_mask * inverse).astype(BF16)
+    loads[1].wait()
     spectrum = spectrum_ref[...].astype(F32)
     spectrum_rows[...] = spectrum
-    cotangent_rows[...] = cotangent_ref[...].astype(F32)
-    band_bf = band_mask.astype(BF16)
-    energy = jnp.zeros((spectrum.shape[0], PAD), F32)
-    for term in split_three(spectrum * spectrum):
-        energy += dot(term, band_bf, NT)
-    energy_ref[...] = jnp.zeros_like(energy_ref)
-    energy_ref[:, :PAD] = energy
 
     quarters = [
         (1 - chip) * 2 + 1 - core,
@@ -214,7 +216,7 @@
     across = [None, None]
     seconds_in = [None, None]
     for item in range(2):
-        loads[item].wait()
+        loads[2 + 2 * item].wait()
         raw, packed = ((split_raw, split_packed), (mask_raw, mask_packed))[item]
         rows_ref, mask_ref = ((spectrum_rows, segment_ref), (cotangent_rows, scaled_ref))[item]
         pack_weight(raw, packed)
@@ -222,12 +224,25 @@
             parts[item, slot] = band_sums(
                 rows_ref, quarters[slot] * frames, mask_ref, packed, masked_ref
             )
-            if item == 0 and slot == 0:
-                pl.semaphore_wait(barrier, len(everyone))
-                for index, peer in enumerate((other_core, other_chip, diagonal)):
-                    energy_copies.append(begin(energy_ref, energies.at[index], peer))
             if slot == 0:
+                if item == 0:
+                    pl.semaphore_wait(barrier, len(everyone))
                 first = begin(parts.at[item, 0], from_core.at[item, 0], other_core)
+                if item == 0:
+                    band_mask = dot(bands, repeat)
+                    inverse = 1.0 / jnp.sum(band_mask, axis=0, keepdims=True)
+                    inverse_ref[...] = inverse
+                    scaled_ref[...] = (segment_mask * inverse).astype(BF16)
+                    loads[3].wait()
+                    cotangent_rows[...] = cotangent_ref[...].astype(F32)
+                    band_bf = band_mask.astype(BF16)
+                    energy = jnp.zeros((spectrum.shape[0], PAD), F32)
+                    for term in split_three(spectrum * spectrum):
+                        energy += dot(term, band_bf, NT)
+                    energy_ref[...] = jnp.zeros_like(energy_ref)
+                    energy_ref[:, :PAD] = energy
+                    for index, peer in enumerate((other_core, other_chip, diagonal)):
+                        energy_copies.append(begin(energy_ref, energies.at[index], peer))
             if slot == 1:
                 first.wait_recv()
                 to_chip[item] = (
@@ -259,8 +274,8 @@
     mine = iota((rows, tokens), 0) == me * frames + iota((rows, tokens), 1) // PAD
     energy = jnp.sum(jnp.where(mine, energy, 0.0), axis=0, keepdims=True)
     in_band = iota((1, tokens), 1) % PAD < BANDS
-    loads[2].wait()
-    loads[3].wait()
+    for copy in loads[5:]:
+        copy.wait()
 
     hidden_in = (jnp.transpose(reduced(0)) * lax.rsqrt(energy + EPSILON)).astype(BF16)
     hidden_in = hidden_in.astype(F32)
@@ -352,17 +367,15 @@
 
     half = grad_ref.shape[0] // 2
     columns = grad_ref.shape[1] // 2
-    left, right = pl.ds(0, columns), pl.ds(columns, columns)
     pair_copy = begin(
         grad_ref.at[pl.ds(pl.multiple_of((1 - core) * half, half), half), :], core_in, other_core
     )
-    to_chip_rows.wait_recv()
-    chip_rows = normed_all.at[(1 - chip) * 2 + core]
-    onward = begin(chip_rows, chip_rows, other_core)
     mask_rows(me)
     pair_copy.wait_recv()
     own = pl.ds(pl.multiple_of(core * half, half), half)
-    pair_sum[...] = (grad_ref[own, :].astype(F32) + core_in[...].astype(F32)).astype(BF16)
+    both_cores = (grad_ref[own, :].astype(F32) + core_in[...].astype(F32)).astype(BF16)
+    pair_sum[0] = both_cores[:, :columns]
+    pair_sum[1] = both_cores[:, columns:]
 
     axes = ((x, x_size, x_peers), (y, y_size, y_peers))
     counts = [half // x_size, half // y_size]
@@ -375,18 +388,21 @@
                 there = pl.ds(pl.multiple_of(lax.rem(at + step + 1, size) * count, count), count)
                 firsts[part].append(
                     begin(
-                        pair_sum.at[there, (left, right)[part]],
+                        pair_sum.at[part, there, :],
                         first_in[part].at[step],
                         peers[step],
                     )
                 )
     to_core_rows.wait_recv()
     mask_rows(chip * 2 + 1 - core)
+    to_chip_rows.wait_recv()
+    chip_rows = normed_all.at[(1 - chip) * 2 + core]
+    onward = begin(chip_rows, chip_rows, other_core)
     for part in range(2):
         at, size, peers = axes[part]
         count = counts[part]
         here = pl.ds(pl.multiple_of(at * count, count), count)
-        total = pair_sum[here, (left, right)[part]].astype(F32)
+        total = pair_sum[part, here, :].astype(F32)
         for step in range(size - 1):
             firsts[part][step].wait_recv()
             total += first_in[part][step].astype(F32)
@@ -426,6 +442,7 @@
         ]
     onward.wait_recv()
     mask_rows((1 - chip) * 2 + 1 - core)
+    drain()
     if z_size > 1:
         total = second_sum[z]
         for step in range(z_size - 1):
@@ -456,38 +473,51 @@
                 begin(second_all[part].at[here, :], second_all[part].at[here, :], peer)
             )
     spread = ([], [])
-    mirrored = []
-    base = core * half
     for part in range(2):
         for copy in backs[part]:
             copy.wait_recv()
         at, size, peers = axes[part]
         count = counts[part]
-        here = pl.ds(pl.multiple_of(base + at * count, count), count)
-        target = gathered.at[here, (left, right)[part]]
+        here = pl.ds(pl.multiple_of(at * count, count), count)
+        target = gathered.at[part, core, here, :]
         for peer in peers:
             spread[part].append(begin(second_all[part], target, peer))
-        gathered[here, (left, right)[part]] = second_all[part][...]
-        mirrored.append(begin(second_all[part], target, other_core))
-    for step in range(max(x_size, y_size) - 1):
-        for part in range(2):
-            at, size, peers = axes[part]
-            if step < size - 1:
-                count = counts[part]
-                spread[part][step].wait_recv()
-                origin = lax.rem(at + size - step - 1, size)
-                here = pl.ds(pl.multiple_of(base + origin * count, count), count)
-                block = gathered.at[here, (left, right)[part]]
-                mirrored.append(begin(block, block, other_core))
+        gathered[part, core, here, :] = second_all[part][...]
+    mirrored = []
+    for part in range(2):
+        for copy in spread[part]:
+            copy.wait_recv()
+        whole = gathered.at[part, core]
+        mirrored.append(begin(whole, whole, other_core))
     for copy in mirrored:
         copy.wait_recv()
-    qkv_out[...] = gathered[:D, :].astype(F32)
+    drain()
+
+
+def store_kernel(gathered_ref, rows_ref, mask_hbm, qkv_hbm, out_hbm, qkv_ref, out_ref, store):
+    copies = [pltpu.make_async_copy(rows_ref, mask_hbm, store.at[0])]
+    copies[0].start()
+    columns = gathered_ref.shape[3]
+    quarter = INNER // 4
+    for block in range(3):
+        here = slice(block * quarter, (block + 1) * quarter)
+        there = slice(block % 2 * quarter, (block % 2 + 1) * quarter)
+        for part in range(2):
+            qkv_ref[here, part * columns : (part + 1) * columns] = gathered_ref[
+                part, block // 2, there, :
+            ].astype(F32)
+        copies.append(
+            pltpu.make_async_copy(qkv_ref.at[here, :], qkv_hbm.at[here, :], store.at[1 + block])
+        )
+        copies[-1].start()
     for block in range(4):
-        out_out[block * quarter : (block + 1) * quarter, :] = gathered[
-            D:, block * D : (block + 1) * D
+        out_ref[block * quarter : (block + 1) * quarter, :] = gathered_ref[
+            block // 2, 1, quarter:, block % 2 * D : (block % 2 + 1) * D
         ].astype(F32)
-    for copy in started:
-        copy.wait_send()
+    copies.append(pltpu.make_async_copy(out_ref, out_hbm, store.at[4]))
+    copies[-1].start()
+    for copy in copies:
+        copy.wait()
 
 
 def rotary_table(tokens):
@@ -516,18 +546,21 @@
         return pltpu.VMEM(shape, dtype)
 
     inside = pl.BlockSpec(memory_space=pltpu.VMEM)
-    anywhere = pl.BlockSpec(memory_space=pl.ANY)
+    outside = pl.BlockSpec(memory_space=pltpu.HBM)
     assign = jnp.transpose(band_assign, (2, 0, 1))
-    return pl.pallas_call(
+    rows, gathered = pl.pallas_call(
         functools.partial(whole_kernel, sizes),
         out_shape=[
             jax.ShapeDtypeStruct((frames, width), F32),
-            jax.ShapeDtypeStruct(qkv_weight.shape, F32),
-            jax.ShapeDtypeStruct(out_weight.shape, F32),
+            jax.ShapeDtypeStruct((2, 2, half, columns), BF16),
         ],
-        in_specs=[inside] * 4 + [anywhere] * 4,
-        out_specs=[inside] * 3,
+        in_specs=[outside] * 8,
+        out_specs=[inside] * 2,
         scratch_shapes=[
+            vmem(frames, width),
+            vmem(frames, width),
+            vmem(*assign.shape, dtype=jnp.int32),
+            vmem(2 * HALF, tokens, dtype=F32),
             vmem(*split_weight.shape),
             vmem(*mask_weight.shape),
             vmem(*qkv_weight.shape),
@@ -553,9 +586,8 @@
             vmem(INNER, 4 * D),
             vmem(4, tokens, D),
             vmem(tokens, 2 * D),
-            vmem(INNER, 4 * D),
             vmem(half, 4 * D),
-            vmem(half, 4 * D),
+            vmem(2, half, columns),
             [
                 vmem(max(x_size - 1, 1), half // x_size, columns),
                 vmem(y_size - 1, half // y_size, columns),
@@ -566,7 +598,7 @@
             vmem(7, 8, D, dtype=F32),
             vmem(8, 8, D, dtype=F32),
             [vmem(half // x_size, columns), vmem(half // y_size, columns)],
-            pltpu.SemaphoreType.DMA((4,)),
+            pltpu.SemaphoreType.DMA((8,)),
             pltpu.SemaphoreType.DMA((copies,)),
             pltpu.SemaphoreType.DMA((copies,)),
         ],
@@ -574,14 +606,37 @@
             vmem_limit_bytes=VMEM_BYTES, collective_id=0, has_side_effects=True
         ),
     )(
-        spectrum,
-        mask_cotangent,
-        assign,
-        jnp.asarray(rotary_table(tokens)),
-        split_weight,
-        mask_weight,
-        qkv_weight,
-        out_weight,
+        *(
+            pltpu.with_memory_space_constraint(operand, pltpu.HBM)
+            for operand in (
+                spectrum,
+                mask_cotangent,
+                assign,
+                jnp.asarray(rotary_table(tokens)),
+                split_weight,
+                mask_weight,
+                qkv_weight,
+                out_weight,
+            )
+        )
+    )
+    return tuple(
+        pl.pallas_call(
+            store_kernel,
+            out_shape=[
+                jax.ShapeDtypeStruct((frames, width), F32),
+                jax.ShapeDtypeStruct(qkv_weight.shape, F32),
+                jax.ShapeDtypeStruct(out_weight.shape, F32),
+            ],
+            in_specs=[inside] * 2,
+            out_specs=[outside] * 3,
+            scratch_shapes=[
+                vmem(*qkv_weight.shape, dtype=F32),
+                vmem(*out_weight.shape, dtype=F32),
+                pltpu.SemaphoreType.DMA((5,)),
+            ],
+            compiler_params=pltpu.CompilerParams(vmem_limit_bytes=VMEM_BYTES // 4),
+        )(gathered, rows)
     )
 
 

time: 79.1 us -> 68.8 us (0.87)
  local copies, waits for them, and re-layouts: 10.6 us -> 0 us
    unnamed x15 -> x0, local copies, waits for them, and re-layouts: 10.6 us -> none
    pallas_call x0 -> x1, Pallas kernels: none -> 1.75 us  [on_device(): pl.pallas_call(store_kernel, out_shape=[jax.ShapeDtypeStruct((frames, wid...]
    pallas_call x1, Pallas kernels: 67.5 us -> 66.2 us  [on_device(): pl.pallas_call(functools.partial(whole_kernel, sizes), out_shape=[jax.Sha...]
where the time goes in v3:
time: 68.8 us
  Pallas kernels  67.9 us (99%)
  between operations  0.8 us (1%)
    pallas_call x1, Pallas kernels, on_device(): pl.pallas_call(functools.partial(whole_kernel, sizes), out_shape=[jax.Sha...  66.2 us
    pallas_call x1, Pallas kernels, on_device(): pl.pallas_call(store_kernel, out_shape=[jax.ShapeDtypeStruct((frames, wid...  1.75 us

profile of v3, /device:TPU:1, one launch (start us, length us, event | category | flops | bytes accessed | tf_op | source)
XLA Modules:
  0.0 68.8 jit_solution(1087986178129669014)
XLA Ops:
  0.6 66.2 %shard_map.103 = (f32[16,2048]{1,0:T(8,128)S(1)}, bf16[2,2,256,768]{3,2,1,0:T(8,128)(2,1)S(1)}) custom-call(bf16[16,2048]{1,0:T(8,128)(2,1)} %spectrum_hbm.1, bf16[16,2048]{1,0:T(8,128)(2,1)} %cotangent_hbm.1, s32[60,2,1024]{2,1,0:T(2,128)} %bitcast.1, f32[64,256]{1,0:T(8,128)} %constant.2.clone.table_hbm, bf16[256,2,8,384]{3,2,1,0:T(8,128)(2,1)} %split_hbm.1, ...), custom_call_target="tpu_custom_call" | custom-call | tf_op jit(solution)/shard_map/pallas_call | solution.py:551
  66.8 1.8 %shard_map.104 = (f32[16,2048]{1,0:T(8,128)}, f32[384,1536]{1,0:T(8,128)}, f32[512,384]{1,0:T(8,128)}) custom-call(bf16[2,2,256,768]{3,2,1,0:T(8,128)(2,1)S(1)} %get-tuple-element.5.gathered_ref, f32[16,2048]{1,0:T(8,128)S(1)} %get-tuple-element.6.rows_ref), custom_call_target="tpu_custom_call" | custom-call | tf_op jit(solution)/shard_map/pallas_call | solution.py:624

commit v4 on v3

--- a/solution.py
+++ b/solution.py
@@ -120,10 +120,17 @@
     heads_ref,
     attended_ref,
     grad_projected_ref,
-    grad_ref,
+    qkv_turned,
+    out_turned,
+    bias_ref,
+    normed_ref,
+    normed_in_other,
+    attended_other,
+    grad_hidden_ref,
+    grad_hidden_other,
+    grad_projected_other,
     normed_all,
     pair_ref,
-    core_in,
     pair_sum,
     first_in,
     first_sum,
@@ -175,6 +182,9 @@
         copy = pltpu.make_async_copy(source, target, load.at[index])
         copy.start()
         loads.append(copy)
+    def far_first(size):
+        return sorted(range(1, size), key=lambda s: -min(s, size - s))
+
     next_index = [0]
     started = []
 
@@ -276,6 +286,11 @@
     in_band = iota((1, tokens), 1) % PAD < BANDS
     for copy in loads[5:]:
         copy.wait()
+    qkv_turned[...] = jnp.transpose(qkv_ref[...])
+    out_turned[...] = jnp.transpose(out_weight_ref[...])
+    key_lane, query_lane = iota((tokens, tokens), 0), iota((tokens, tokens), 1)
+    allowed = (key_lane // PAD == query_lane // PAD) & (key_lane % PAD < BANDS)
+    bias_ref[...] = jnp.where(allowed, 0.0, -1e30)
 
     hidden_in = (jnp.transpose(reduced(0)) * lax.rsqrt(energy + EPSILON)).astype(BF16)
     hidden_in = hidden_in.astype(F32)
@@ -283,12 +298,11 @@
         hidden_in
         * lax.rsqrt(jnp.mean(hidden_in * hidden_in, axis=0, keepdims=True) + EPSILON)
     ).astype(BF16)
-    projected = dot(qkv_ref[...], normed_in, TN)
+    normed_ref[...] = normed_in
+    swaps = [begin(normed_ref, normed_in_other, other_core)]
+    projected = dot(qkv_turned[...], normed_in)
     cos, sin = table_ref[:HALF, :], table_ref[HALF:, :]
     scale = HEAD_DIM**-0.5
-    key_lane, query_lane = iota((tokens, tokens), 0), iota((tokens, tokens), 1)
-    allowed = (key_lane // PAD == query_lane // PAD) & (key_lane % PAD < BANDS)
-    bias = jnp.where(allowed, 0.0, -1e30)
     for head in range(HEADS):
         for part in range(2):
             base = part * INNER + head * HEAD_DIM
@@ -306,14 +320,18 @@
         return heads_ref[base : base + HEAD_DIM, :]
 
     for head in range(HEADS):
-        scores = dot(part_of(1, head), part_of(0, head), TN) + bias
+        scores = dot(part_of(1, head), part_of(0, head), TN) + bias_ref[...]
         powers = jnp.exp(scores - jnp.max(scores, axis=0, keepdims=True))
         probs = powers / jnp.sum(powers, axis=0, keepdims=True)
         probs_ref[head] = probs
         attended_ref[head * HEAD_DIM : (head + 1) * HEAD_DIM, :] = dot(
             part_of(2, head), probs.astype(BF16)
         ).astype(BF16)
-    mixed = dot(out_weight_ref[...], attended_ref[...], TN)
+    inner_half = INNER // 2
+    own_inner = pl.ds(pl.multiple_of(core * inner_half, inner_half), inner_half)
+    other_inner = pl.ds(pl.multiple_of((1 - core) * inner_half, inner_half), inner_half)
+    swaps.append(begin(attended_ref.at[other_inner, :], attended_other, other_core))
+    mixed = dot(out_turned[...], attended_ref[...])
     hidden_out = (hidden_in + mixed).astype(BF16).astype(F32)
     inverse = lax.rsqrt(jnp.mean(hidden_out * hidden_out, axis=0, keepdims=True) + EPSILON)
     normed_out = jnp.where(in_band, hidden_out * inverse, 0.0)
@@ -327,12 +345,8 @@
         inverse * upstream - hidden_out * (inverse * inverse * inverse) * inner
     ).astype(BF16)
     grad_attended = dot(out_weight_ref[...], grad_hidden).astype(BF16)
-    out_grad = dot(attended_ref[...], grad_hidden, NT).astype(BF16)
-    quarter = INNER // 4
-    for block in range(4):
-        grad_ref[D:, block * D : (block + 1) * D] = out_grad[
-            block * quarter : (block + 1) * quarter
-        ]
+    grad_hidden_ref[...] = grad_hidden
+    swaps.append(begin(grad_hidden_ref, grad_hidden_other, other_core))
     for head in range(HEADS):
         probs = probs_ref[head]
         grad_head = grad_attended[head * HEAD_DIM : (head + 1) * HEAD_DIM]
@@ -351,7 +365,12 @@
             ).astype(BF16)
         base = 2 * INNER + head * HEAD_DIM
         grad_projected_ref[base : base + HEAD_DIM, :] = grad_values.astype(BF16)
-    grad_ref[:D, :] = dot(normed_in, grad_projected_ref[...], NT).astype(BF16)
+    columns = 3 * INNER // 2
+    own_columns = pl.ds(pl.multiple_of(core * columns, columns), columns)
+    other_columns = pl.ds(pl.multiple_of((1 - core) * columns, columns), columns)
+    last_swap = begin(
+        grad_projected_ref.at[other_columns, :], grad_projected_other, other_core
+    )
 
     def mask_rows(quarter):
         normed = normed_all[quarter]
@@ -365,33 +384,35 @@
                 jnp.sum(block * mask, axis=0, keepdims=True) * inverse_ref[...]
             )
 
-    half = grad_ref.shape[0] // 2
-    columns = grad_ref.shape[1] // 2
-    pair_copy = begin(
-        grad_ref.at[pl.ds(pl.multiple_of((1 - core) * half, half), half), :], core_in, other_core
+    half = INNER // 2
+    quarter = INNER // 4
+    for copy in swaps:
+        copy.wait_recv()
+    out_grad = dot(attended_ref[own_inner, :], grad_hidden, NT) + dot(
+        attended_other[...], grad_hidden_other[...], NT
     )
+    for block in range(2):
+        pair_sum[1, quarter:, block * D : (block + 1) * D] = out_grad[
+            block * quarter : (block + 1) * quarter
+        ].astype(BF16)
+    own_grad = dot(normed_in, grad_projected_ref[own_columns, :], NT)
     mask_rows(me)
-    pair_copy.wait_recv()
-    own = pl.ds(pl.multiple_of(core * half, half), half)
-    both_cores = (grad_ref[own, :].astype(F32) + core_in[...].astype(F32)).astype(BF16)
-    pair_sum[0] = both_cores[:, :columns]
-    pair_sum[1] = both_cores[:, columns:]
+    last_swap.wait_recv()
+    own_grad = (own_grad + dot(normed_in_other[...], grad_projected_other[...], NT)).astype(BF16)
+    pair_sum[0] = own_grad[:half]
+    pair_sum[1, :quarter, :] = own_grad[half:]
 
     axes = ((x, x_size, x_peers), (y, y_size, y_peers))
     counts = [half // x_size, half // y_size]
-    firsts = ([], [])
-    for step in range(max(x_size, y_size) - 1):
+    firsts = ({}, {})
+    for step in far_first(4):
         for part in range(2):
             at, size, peers = axes[part]
-            if step < size - 1:
+            if step < size:
                 count = counts[part]
-                there = pl.ds(pl.multiple_of(lax.rem(at + step + 1, size) * count, count), count)
-                firsts[part].append(
-                    begin(
-                        pair_sum.at[part, there, :],
-                        first_in[part].at[step],
-                        peers[step],
-                    )
+                there = pl.ds(pl.multiple_of(lax.rem(at + step, size) * count, count), count)
+                firsts[part][step] = begin(
+                    pair_sum.at[part, there, :], first_in[part].at[step - 1], peers[step - 1]
                 )
     to_core_rows.wait_recv()
     mask_rows(chip * 2 + 1 - core)
@@ -403,21 +424,21 @@
         count = counts[part]
         here = pl.ds(pl.multiple_of(at * count, count), count)
         total = pair_sum[part, here, :].astype(F32)
-        for step in range(size - 1):
+        for step in range(1, size):
             firsts[part][step].wait_recv()
-            total += first_in[part][step].astype(F32)
+            total += first_in[part][step - 1].astype(F32)
         first_sum[part][...] = total.astype(BF16)
 
     last_rows = half // (x_size * y_size)
-    seconds = ([], [])
+    seconds = ({}, {})
     for part in range(2):
         at, size, peers = axes[1 - part]
-        for step in range(size - 1):
+        for step in far_first(size):
             there = pl.ds(
-                pl.multiple_of(lax.rem(at + step + 1, size) * last_rows, last_rows), last_rows
+                pl.multiple_of(lax.rem(at + step, size) * last_rows, last_rows), last_rows
             )
-            seconds[part].append(
-                begin(first_sum[part].at[there, :], second_in[part].at[step], peers[step])
+            seconds[part][step] = begin(
+                first_sum[part].at[there, :], second_in[part].at[step - 1], peers[step - 1]
             )
     mask_rows((1 - chip) * 2 + core)
     chunk_rows, chunk_columns = 8, columns // 2
@@ -425,9 +446,9 @@
         at, size, peers = axes[1 - part]
         here = pl.ds(pl.multiple_of(at * last_rows, last_rows), last_rows)
         total = first_sum[part][here, :].astype(F32)
-        for step in range(size - 1):
+        for step in range(1, size):
             seconds[part][step].wait_recv()
-            total += second_in[part][step].astype(F32)
+            total += second_in[part][step - 1].astype(F32)
         if z_size == 1:
             second_all[part][here, :] = total.astype(BF16)
         else:
@@ -436,20 +457,22 @@
                 second_sum[part * 4 + block] = total[r : r + chunk_rows, c : c + chunk_columns]
 
     if z_size > 1:
-        depths = [
-            begin(second_sum.at[lax.rem(z + s, z_size)], depth_in.at[s - 1], z_peers[s - 1])
-            for s in range(1, z_size)
-        ]
+        depths = {
+            s: begin(second_sum.at[lax.rem(z + s, z_size)], depth_in.at[s - 1], z_peers[s - 1])
+            for s in far_first(z_size)
+        }
     onward.wait_recv()
     mask_rows((1 - chip) * 2 + 1 - core)
     drain()
     if z_size > 1:
         total = second_sum[z]
-        for step in range(z_size - 1):
+        for step in range(1, z_size):
             depths[step].wait_recv()
-            total += depth_in[step]
+            total += depth_in[step - 1]
         depth_all[z] = total
-        backs = [begin(depth_all.at[z], depth_all.at[z], peer) for peer in z_peers]
+        backs = [
+            begin(depth_all.at[z], depth_all.at[z], z_peers[s - 1]) for s in far_first(z_size)
+        ]
         for copy in backs:
             copy.wait_recv()
         for part in range(2):
@@ -468,10 +491,9 @@
     for part in range(2):
         at, size, peers = axes[1 - part]
         here = pl.ds(pl.multiple_of(at * last_rows, last_rows), last_rows)
-        for peer in peers:
-            backs[part].append(
-                begin(second_all[part].at[here, :], second_all[part].at[here, :], peer)
-            )
+        for step in far_first(size):
+            block = second_all[part].at[here, :]
+            backs[part].append(begin(block, block, peers[step - 1]))
     spread = ([], [])
     for part in range(2):
         for copy in backs[part]:
@@ -480,8 +502,8 @@
         count = counts[part]
         here = pl.ds(pl.multiple_of(at * count, count), count)
         target = gathered.at[part, core, here, :]
-        for peer in peers:
-            spread[part].append(begin(second_all[part], target, peer))
+        for step in far_first(size):
+            spread[part].append(begin(second_all[part], target, peers[step - 1]))
         gathered[part, core, here, :] = second_all[part][...]
     mirrored = []
     for part in range(2):
@@ -489,9 +511,9 @@
             copy.wait_recv()
         whole = gathered.at[part, core]
         mirrored.append(begin(whole, whole, other_core))
+    drain()
     for copy in mirrored:
         copy.wait_recv()
-    drain()
 
 
 def store_kernel(gathered_ref, rows_ref, mask_hbm, qkv_hbm, out_hbm, qkv_ref, out_ref, store):
@@ -502,9 +524,9 @@
     for block in range(3):
         here = slice(block * quarter, (block + 1) * quarter)
         there = slice(block % 2 * quarter, (block % 2 + 1) * quarter)
-        for part in range(2):
-            qkv_ref[here, part * columns : (part + 1) * columns] = gathered_ref[
-                part, block // 2, there, :
+        for core in range(2):
+            qkv_ref[here, core * columns : (core + 1) * columns] = gathered_ref[
+                block // 2, core, there, :
             ].astype(F32)
         copies.append(
             pltpu.make_async_copy(qkv_ref.at[here, :], qkv_hbm.at[here, :], store.at[1 + block])
@@ -512,7 +534,7 @@
         copies[-1].start()
     for block in range(4):
         out_ref[block * quarter : (block + 1) * quarter, :] = gathered_ref[
-            block // 2, 1, quarter:, block % 2 * D : (block % 2 + 1) * D
+            1, block // 2, quarter:, block % 2 * D : (block % 2 + 1) * D
         ].astype(F32)
     copies.append(pltpu.make_async_copy(out_ref, out_hbm, store.at[4]))
     copies[-1].start()
@@ -583,10 +605,17 @@
             vmem(3 * INNER, tokens),
             vmem(INNER, tokens),
             vmem(3 * INNER, tokens),
-            vmem(INNER, 4 * D),
+            vmem(3 * INNER, D),
+            vmem(D, INNER),
+            vmem(tokens, tokens, dtype=F32),
+            vmem(D, tokens),
+            vmem(D, tokens),
+            vmem(INNER // 2, tokens),
+            vmem(D, tokens),
+            vmem(D, tokens),
+            vmem(3 * INNER // 2, tokens),
             vmem(4, tokens, D),
             vmem(tokens, 2 * D),
-            vmem(half, 4 * D),
             vmem(2, half, columns),
             [
                 vmem(max(x_size - 1, 1), half // x_size, columns),

time: 68.8 us -> 67.3 us (0.978)
  Pallas kernels: 67.9 us -> 66.4 us
    pallas_call x1, Pallas kernels: 66.2 us -> 64.6 us  [on_device(): pl.pallas_call(functools.partial(whole_kernel, sizes), out_shape=[jax.Sha...]
where the time goes in v4:
time: 67.3 us; the launch traced here: 67.2 us
  Pallas kernels  66.4 us (99%)
  between operations  0.8 us (1%)
    pallas_call x1, Pallas kernels, on_device(): pl.pallas_call(functools.partial(whole_kernel, sizes), out_shape=[jax.Sha...  64.6 us
    pallas_call x1, Pallas kernels, on_device(): pl.pallas_call(store_kernel, out_shape=[jax.ShapeDtypeStruct((frames, wid...  1.75 us

profile of v4, /device:TPU:1, one launch (start us, length us, event | category | flops | bytes accessed | tf_op | source)
XLA Modules:
  0.0 67.2 jit_solution(17735862771707508079)
XLA Ops:
  0.6 64.6 %shard_map.103 = (f32[16,2048]{1,0:T(8,128)S(1)}, bf16[2,2,256,768]{3,2,1,0:T(8,128)(2,1)S(1)}) custom-call(bf16[16,2048]{1,0:T(8,128)(2,1)} %spectrum_hbm.1, bf16[16,2048]{1,0:T(8,128)(2,1)} %cotangent_hbm.1, s32[60,2,1024]{2,1,0:T(2,128)} %bitcast.1, f32[64,256]{1,0:T(8,128)} %constant.2.clone.table_hbm, bf16[256,2,8,384]{3,2,1,0:T(8,128)(2,1)} %split_hbm.1, ...), custom_call_target="tpu_custom_call" | custom-call | tf_op jit(solution)/shard_map/pallas_call | solution.py:573
  65.3 1.8 %shard_map.104 = (f32[16,2048]{1,0:T(8,128)}, f32[384,1536]{1,0:T(8,128)}, f32[512,384]{1,0:T(8,128)}) custom-call(bf16[2,2,256,768]{3,2,1,0:T(8,128)(2,1)S(1)} %get-tuple-element.5.gathered_ref, f32[16,2048]{1,0:T(8,128)S(1)} %get-tuple-element.6.rows_ref), custom_call_target="tpu_custom_call" | custom-call | tf_op jit(solution)/shard_map/pallas_call | solution.py:653

commit v5 on v4

--- a/solution.py
+++ b/solution.py
@@ -322,7 +322,7 @@
     for head in range(HEADS):
         scores = dot(part_of(1, head), part_of(0, head), TN) + bias_ref[...]
         powers = jnp.exp(scores - jnp.max(scores, axis=0, keepdims=True))
-        probs = powers / jnp.sum(powers, axis=0, keepdims=True)
+        probs = powers * (1.0 / jnp.sum(powers, axis=0, keepdims=True))
         probs_ref[head] = probs
         attended_ref[head * HEAD_DIM : (head + 1) * HEAD_DIM, :] = dot(
             part_of(2, head), probs.astype(BF16)

time: 67.3 us -> 67.3 us (level)
  no operation moved by 1% of the time
where the time goes in v5:
time: 67.3 us; the launch traced here: 67.2 us
  Pallas kernels  66.4 us (99%)
  between operations  0.8 us (1%)
    pallas_call x1, Pallas kernels, on_device(): pl.pallas_call(functools.partial(whole_kernel, sizes), out_shape=[jax.Sha...  64.6 us
    pallas_call x1, Pallas kernels, on_device(): pl.pallas_call(store_kernel, out_shape=[jax.ShapeDtypeStruct((frames, wid...  1.75 us

profile of v5, /device:TPU:1, one launch (start us, length us, event | category | flops | bytes accessed | tf_op | source)
XLA Modules:
  0.0 67.2 jit_solution(17735862771707508079)
XLA Ops:
  0.6 64.6 %shard_map.103 = (f32[16,2048]{1,0:T(8,128)S(1)}, bf16[2,2,256,768]{3,2,1,0:T(8,128)(2,1)S(1)}) custom-call(bf16[16,2048]{1,0:T(8,128)(2,1)} %spectrum_hbm.1, bf16[16,2048]{1,0:T(8,128)(2,1)} %cotangent_hbm.1, s32[60,2,1024]{2,1,0:T(2,128)} %bitcast.1, f32[64,256]{1,0:T(8,128)} %constant.2.clone.table_hbm, bf16[256,2,8,384]{3,2,1,0:T(8,128)(2,1)} %split_hbm.1, ...), custom_call_target="tpu_custom_call" | custom-call | tf_op jit(solution)/shard_map/pallas_call | solution.py:573
  65.3 1.8 %shard_map.104 = (f32[16,2048]{1,0:T(8,128)}, f32[384,1536]{1,0:T(8,128)}, f32[512,384]{1,0:T(8,128)}) custom-call(bf16[2,2,256,768]{3,2,1,0:T(8,128)(2,1)S(1)} %get-tuple-element.5.gathered_ref, f32[16,2048]{1,0:T(8,128)S(1)} %get-tuple-element.6.rows_ref), custom_call_target="tpu_custom_call" | custom-call | tf_op jit(solution)/shard_map/pallas_call | solution.py:653
